TPU v7x, 32 devices: a whole 2x2x4 slice. The times are simulated.
32 devices in a mesh: sec: 2 (over x), dev: 16 (over z, y, core).
Axes of the slice: x: 2, y: 2, z: 4, core: 2. Of those that a mesh axis runs over, the one named last changes fastest.
Arguments:
- queries: bfloat16 [32, 8192], P('dev', 'sec'), may hold values from -24 to 24
- cache_keys: bfloat16 [32, 4, 512, 128], P('dev', 'sec'), may hold values from -24 to 24
- cache_values: bfloat16 [32, 4, 512, 128], P('dev', 'sec'), may hold values from -48 to 48
- lengths: int32 [32], P('dev'), may hold values from 2 to 512, as said below
- out_proj: bfloat16 [4096, 8192], P('dev', 'sec'), may hold values from -0.0625 to 0.0625
- residual: bfloat16 [32, 4096], P(None, 'dev'), may hold values from -3 to 3
- norm_gain: bfloat16 [4096], replicated, may hold values from 0.5 to 1.5
- expert_ids: int32 [32, 8], replicated, may hold values from 0 to 15, all different within a row; in each aligned block of 32 rows (0 to 31, 32 to 63, ...) at most 32 rows name the same one
- gate_weights: float32 [32, 8], replicated, may hold values from 0.5 to 1.5
- owners: int32 [16], replicated, may hold values from 0 to 15, each once
- gate_proj: bfloat16 [16, 768, 4096], P('dev', 'sec'), may hold values from -0.09375 to 0.09375
- up_proj: bfloat16 [16, 768, 4096], P('dev', 'sec'), may hold values from -0.09375 to 0.09375
- down_proj: bfloat16 [16, 768, 4096], P('dev', 'sec'), may hold values from -0.21875 to 0.21875
Outputs:
- output: bfloat16 [32, 4096], P(None, 'dev')
Inputs may be any that keep to these rules, and one draw needn't show every extreme that they name: Row r's cache holds lengths[r] live positions from position 0; some row holds exactly 512. `expert_ids`: each row names 8 different experts; over all 32 rows no expert is named more than 32 times, a bound that some block reaches. Each index appears once; expert e's projections stand at index owners[e] of the expert projections.
All inputs are finite; a program needn't handle non-finite values.
Results may differ from a plain program's by a relative error of at most 0.009.
Values may be sent and summed in bfloat16 or wider, within the bound.
A program may use at most 64 MiB of HBM per device.

v0:
```python
import math

import jax
import jax.numpy as jnp
from jax import lax
from jax.sharding import PartitionSpec as P

epsilon = 1e-05


def slot_targets(expert_ids, owners, capacity):
    experts = owners.shape[0]
    flat_ids = expert_ids.reshape(-1)
    one_hot = (flat_ids[:, None] == jnp.arange(experts, dtype=jnp.int32)[None, :]).astype(jnp.int32)
    before = jnp.cumsum(one_hot, axis=0) - one_hot
    position = jnp.sum(before * one_hot, axis=1)
    holder = jnp.sum(one_hot * owners[None, :], axis=1)
    return (holder * capacity + position).reshape(expert_ids.shape)


def routing_tables(expert_ids, gate_weights, owners, capacity):
    target = slot_targets(expert_ids, owners, capacity)
    places = jnp.arange(owners.shape[0] * capacity, dtype=jnp.int32)
    matched = target[None, :, :] == places[:, None, None]
    sending = jnp.any(matched, axis=2)
    weighting = jnp.sum(
        jnp.where(matched, gate_weights[None, :, :], jnp.zeros_like(gate_weights)[None, :, :]),
        axis=2,
    )
    return (sending, weighting)


def times_transpose(left, right):
    return lax.dot_general(
        left, right, (((1,), (1,)), ((), ())), preferred_element_type=jnp.float32
    )


def attend(queries, cache_keys, cache_values, lengths):
    rows, kv_heads, key_span, head_dim = cache_keys.shape
    group_size = queries.shape[1] // (kv_heads * head_dim)
    grouped = queries.reshape(rows, kv_heads, group_size, head_dim)
    scores = jnp.einsum(
        "rkgd,rktd->rkgt", grouped, cache_keys, preferred_element_type=jnp.float32
    ) / math.sqrt(head_dim)
    live_mask = (
        jnp.arange(key_span, dtype=jnp.int32)[None, None, None, :] < lengths[:, None, None, None]
    )
    scores = jnp.where(live_mask, scores, -jnp.inf)
    row_top = jnp.max(scores, axis=-1, keepdims=True)
    raised = jnp.exp(scores - row_top)
    soft_weight = (raised / jnp.sum(raised, axis=-1, keepdims=True)).astype(jnp.bfloat16)
    head_out = jnp.einsum(
        "rkgt,rktd->rkgd", soft_weight, cache_values, preferred_element_type=jnp.float32
    )
    return head_out.astype(jnp.bfloat16).reshape(rows, -1)


def root_norm(arrived, norm_gain):
    square_mean = jnp.mean(arrived * arrived, axis=-1, keepdims=True)
    return (arrived * lax.rsqrt(square_mean + epsilon) * norm_gain.astype(jnp.float32)).astype(
        jnp.bfloat16
    )


def expert_ffn(normed, gate_w, up_w, down_w):
    gate_act = times_transpose(normed, gate_w)
    up_act = times_transpose(normed, up_w)
    hidden = (jax.nn.silu(gate_act) * up_act).astype(jnp.bfloat16)
    return jnp.dot(hidden, down_w, preferred_element_type=jnp.float32)


def shards(
    queries,
    cache_keys,
    cache_values,
    lengths,
    out_proj,
    residual,
    norm_gain,
    expert_ids,
    gate_weights,
    owners,
    gate_proj,
    up_proj,
    down_proj,
):
    head_out = attend(queries, cache_keys, cache_values, lengths)
    attention_part = times_transpose(lax.all_gather(head_out, "dev", axis=0, tiled=True), out_proj)
    rows_all, top_count = expert_ids.shape
    experts = owners.shape[0]
    capacity = min(rows_all, 3 * top_count * rows_all // experts)
    col_count = out_proj.shape[0]
    sending, weighting = routing_tables(expert_ids, gate_weights, owners, capacity)
    residual_wide = residual.astype(jnp.float32)
    attention_out = lax.psum(attention_part, "sec")
    hidden_in = (residual_wide + attention_out).astype(jnp.bfloat16)
    outbound = jnp.dot(sending.astype(jnp.bfloat16), hidden_in, preferred_element_type=jnp.float32)
    outbound = outbound.astype(jnp.bfloat16).reshape(experts, capacity, col_count)
    inbound = lax.all_to_all(outbound, "dev", split_axis=0, concat_axis=2, tiled=True)
    arrived = inbound[0].astype(jnp.float32)
    normed = root_norm(arrived, norm_gain)
    expert_out = expert_ffn(normed, gate_proj[0], up_proj[0], down_proj[0])
    place_weight = jnp.sum(weighting, axis=1)
    own_weight = lax.dynamic_slice_in_dim(
        place_weight, lax.axis_index("dev") * capacity, capacity, 0
    )
    weighted = (expert_out * own_weight[:, None]).astype(jnp.bfloat16)
    returned = lax.all_to_all(
        weighted.reshape(1, capacity, weighted.shape[1]),
        "dev",
        split_axis=2,
        concat_axis=0,
        tiled=True,
    )
    moe = jnp.dot(
        sending.T.astype(jnp.bfloat16),
        returned.reshape(-1, col_count),
        preferred_element_type=jnp.float32,
    )
    summed = lax.psum(moe, "sec")
    return (residual_wide + attention_out + summed).astype(jnp.bfloat16)


def solution(mesh):
    in_specs = (
        P("dev", "sec"),
        P("dev", "sec", None, None),
        P("dev", "sec", None, None),
        P("dev"),
        P("dev", "sec"),
        P(None, "dev"),
        P(),
        P(),
        P(),
        P(),
        P("dev", "sec", None),
        P("dev", "sec", None),
        P("dev", "sec", None),
    )
    out_specs = P(None, "dev")
    return jax.shard_map(shards, mesh=mesh, in_specs=in_specs, out_specs=out_specs, check_vma=False)
```

profile of v0, /device:TPU:0, one launch (start us, length us, event | category | flops | bytes accessed | tf_op | source)
XLA Modules:
  0.0 130.4 jit_solution(2785937166758745142)
XLA Ops:
  0.0 0.9 copy.35
  1.1 0.7 iota_compare_fusion.3
  1.8 0.6 reduce-window.6
  2.7 0.8 select_reduce_fusion.1
  3.7 0.7 copy.44
  4.5 1.3 fusion.9
  5.9 1.3 convolution_convert_fusion.1
  7.3 25.2 %all-gather = bf16[16,2,4096]{2,1,0:T(2,128)(2,1)} all-gather(bf16[1,2,4096]{2,1,0:T(2,128)(2,1)S(1)} %reshape.120), channel_id=1, replica_groups=mesh['sec'=2,'dev'=16] {'dev'}, dimensions={0}, use_global_device_ids=true | all-gather | bytes 278528 | tf_op jit(solution)/shard_map/all_gather | solution.py:89
  32.5 1.0 reshape.121
  33.5 2.3 %fusion.41 = f32[32,256]{1,0:T(8,128)S(1)} fusion(bf16[32,4096]{1,0:T(8,128)(2,1)S(1)} %reshape.121, bf16[256,4096]{1,0:T(8,128)(2,1)} %param.17), kind=kOutput, calls=%fused_computation.55 | convolution fusion | flops 67108864 | bytes 2392064 | tf_op jit(solution)/shard_map/dot_general | solution.py:34
  35.9 8.3 %psum.14 = f32[32,256]{1,0:T(8,128)S(1)} all-reduce(f32[32,256]{1,0:T(8,128)S(1)} %fusion.41), channel_id=1, replica_groups=mesh['sec'=2,'dev'=16] {'sec'}, use_global_device_ids=true, to_apply=%region_2.3 | all-reduce | flops 8192 | bytes 65536 | tf_op jit(solution)/shard_map/psum | solution.py:96
  44.2 1.0 convolution_convert_fusion
  45.2 3.5 %all-to-all-start = ((bf16[16,32,256]{2,1,0:T(8,128)(2,1)}), bf16[16,32,256]{2,1,0:T(8,128)(2,1)S(1)}, u32[]{:S(2)}, u32[]{:S(2)}) async-start(bf16[16,32,256]{2,1,0:T(8,128)(2,1)} %bitcast.85), calls=%async_computation | async-start | bytes 524288 | tf_op jit(solution)/shard_map/all_to_all | solution.py:100
  49.1 9.7 %all-to-all-done = bf16[16,32,256]{2,1,0:T(8,128)(2,1)S(1)} async-done(((bf16[16,32,256]{2,1,0:T(8,128)(2,1)}), bf16[16,32,256]{2,1,0:T(8,128)(2,1)S(1)}, u32[]{:S(2)}, u32[]{:S(2)}) %all-to-all-start) | async-done | bytes 262176 | tf_op jit(solution)/shard_map/all_to_all | solution.py:100
  59.1 2.9 %fusion.6 = f32[32,384]{1,0:T(8,128)S(1)} fusion(bf16[32,4096]{1,0:T(8,128)(2,1)S(1)} %bitcast.82, bf16[1,384,4096]{2,1,0:T(8,128)(2,1)} %param.23), kind=kOutput, calls=%fused_computation.7 | convolution fusion | flops 100663296 | bytes 3457024 | tf_op jit(solution)/shard_map/dot_general | solution.py:34
  62.0 4.6 %fusion.2 = bf16[1,32,4096]{2,1,0:T(8,128)(2,1)} fusion(bf16[1,384,4096]{2,1,0:T(8,128)(2,1)S(1)} %copy-done, bf16[32,4096]{1,0:T(8,128)(2,1)S(1)} %bitcast.83, bf16[1,384,4096]{2,1,0:T(8,128)(2,1)} %param.24, f32[32]{0:T(128)S(1)} %dynamic_slice.3, f32[32,384]{1,0:T(8,128)S(1)} %fusion.6), kind=kOutput, calls=%fused_computation.3 | convolution fusion | flops 201662464 | bytes 6865024 | tf_op jit(solution)/shard_map/dot_general | solution.py:70
  66.7 5.0 %copy.40 = bf16[1,32,4096]{1,0,2:T(2,128)(2,1)} copy(bf16[1,32,4096]{2,1,0:T(8,128)(2,1)} %fusion.2) | data formatting | bytes 524288 | tf_op jit(solution)/shard_map/reshape | solution.py:110
  72.2 24.4 %reduce.5 = bf16[4096,32]{1,0:T(8,128)(2,1)} reduce(bf16[4096,1,32]{2,1,0:T(2,128)(2,1)} %bitcast.81, bf16[]{:T(256)} %broadcast.83), dimensions={1}, to_apply=%bitcast.59.reduce_sub_computation | reduce | bytes 524290
  96.7 2.5 %reshape.124 = bf16[16,2,4096]{2,1,0:T(2,128)(2,1)S(1)} reshape(bf16[4096,32]{1,0:T(8,128)(2,1)} %reduce.5) | data formatting | bytes 524288
  99.1 13.3 %all_to_all.24 = bf16[16,2,4096]{2,1,0:T(2,128)(2,1)} all-to-all(bf16[16,2,4096]{2,1,0:T(2,128)(2,1)S(1)} %reshape.124), channel_id=1, replica_groups=mesh['sec'=2,'dev'=16] {'dev'}, dimensions={0} | all-to-all | bytes 524288 | tf_op jit(solution)/shard_map/all_to_all | solution.py:109
  112.4 5.2 %reshape.125 = bf16[4096,1,32]{2,1,0:T(2,128)(2,1)} reshape(bf16[16,2,4096]{2,1,0:T(2,128)(2,1)} %all_to_all.24) | data formatting | bytes 524288
  117.6 4.5 %copy.41 = bf16[1,32,4096]{2,1,0:T(8,128)(2,1)S(1)} copy(bf16[1,32,4096]{1,0,2:T(2,128)(2,1)} %bitcast.80) | data formatting | bytes 524288 | tf_op jit(solution)/shard_map/all_to_all | solution.py:109
  122.4 7.4 %psum.15 = f32[32,256]{1,0:T(8,128)S(1)} all-reduce(f32[32,256]{1,0:T(8,128)S(1)} %fusion.42), channel_id=1, replica_groups=mesh['sec'=2,'dev'=16] {'sec'}, use_global_device_ids=true, to_apply=%region_10.11 | all-reduce | flops 8192 | bytes 65536 | tf_op jit(solution)/shard_map/psum | solution.py:121
  129.8 0.6 add_convert_fusion
  (32 shorter events, 2.4 us)
Async XLA Ops:
  0.0 62.0 %copy-start = (bf16[1,384,4096]{2,1,0:T(8,128)(2,1)S(1)}, bf16[1,384,4096]{2,1,0:T(8,128)(2,1)}, u32[]{:S(2)}) copy-start(bf16[1,384,4096]{2,1,0:T(8,128)(2,1)} %param.25) | copy-start | bytes 9437188
  0.0 44.2 %copy-start.1 = (bf16[32,256]{1,0:T(8,128)(2,1)S(1)}, bf16[32,256]{1,0:T(8,128)(2,1)}, u32[]{:S(2)}) copy-start(bf16[32,256]{1,0:T(8,128)(2,1)} %param.18) | copy-start | bytes 49156
  0.0 48.8 %copy-start.2 = (bf16[4096]{0:T(1024)(128)(2,1)S(1)}, bf16[4096]{0:T(1024)(128)(2,1)}, u32[]{:S(2)}) copy-start(bf16[4096]{0:T(1024)(128)(2,1)} %param.19) | copy-start | bytes 24580
  0.0 48.8 %copy-start.3 = (f32[32,8]{0,1:T(8,128)S(1)}, f32[32,8]{0,1:T(8,128)}, u32[]{:S(2)}) copy-start(f32[32,8]{0,1:T(8,128)} %param.21) | copy-start | bytes 3076
  45.2 13.5 %all-to-all-start = ((bf16[16,32,256]{2,1,0:T(8,128)(2,1)}), bf16[16,32,256]{2,1,0:T(8,128)(2,1)S(1)}, u32[]{:S(2)}, u32[]{:S(2)}) async-start(bf16[16,32,256]{2,1,0:T(8,128)(2,1)} %bitcast.85), calls=%async_computation | async-start | bytes 524288 | tf_op jit(solution)/shard_map/all_to_all | solution.py:100
where the time goes:
time: 132 us; the launch traced here: 130 us
  blocking collectives  54.3 us (41%)
  other arithmetic  28.1 us (21%)
  local copies, waits for them, and re-layouts  21.2 us (16%)
  matrix products  13.6 us (10%)
  waiting for transfers between devices  9.66 us (7%)
  starting transfers between devices  3.53 us (3%)
    all_gather x1, blocking collectives, shards(): lax.all_gather(head_out, 'dev', axis=0, tiled=True)  25.2 us
    unnamed x2, other arithmetic  24.6 us
    all_to_all x1, blocking collectives, shards(): lax.all_to_all(weighted.reshape(1, capacity, weighted.shape[1]), 'dev', s...  13.3 us
    unnamed x18, local copies, waits for them, and re-layouts  11 us
    all_to_all x1, waiting for transfers between devices, shards(): lax.all_to_all(outbound, 'dev', split_axis=0, concat_axis=2, tiled=True)  9.66 us
    psum x1, blocking collectives, shards(): attention_out = lax.psum(attention_part, 'sec')  8.35 us
    psum x1, blocking collectives, shards(): summed = lax.psum(moe, 'sec')  7.39 us
    dot_general x2, matrix products, times_transpose(): lax.dot_general(left, right, (((1,), (1,)), ((), ())), preferred_element_...  5.23 us
  transfers between devices with their start and end apart: 1, of which 1 were waited for; matrix products, arithmetic and copies ran while one was open for 0% of the time, Pallas kernels for 0%

commit v1 on v0

--- a/solution.py
+++ b/solution.py
@@ -1,11 +1,15 @@
+import functools
 import math
 
 import jax
 import jax.numpy as jnp
 from jax import lax
+from jax.experimental import pallas as pl
+from jax.experimental.pallas import tpu as pltpu
 from jax.sharding import PartitionSpec as P
 
 epsilon = 1e-05
+MESH = pl.DeviceIdType.MESH
 
 
 def slot_targets(expert_ids, owners, capacity):
@@ -122,6 +126,311 @@
     return (residual_wide + attention_out + summed).astype(jnp.bfloat16)
 
 
+def fused_kernel(
+    n_dev,
+    queries,
+    lengths,
+    residual,
+    norm_gain,
+    expert_ids,
+    gate_weights,
+    owners,
+    keys_hbm,
+    values_hbm,
+    out_proj_hbm,
+    gate_hbm,
+    up_hbm,
+    down_hbm,
+    output,
+    keys,
+    values,
+    out_proj,
+    gate_w,
+    up_w,
+    down_w,
+    query_rows,
+    heads_out,
+    heads_in,
+    heads_wide,
+    part_out,
+    part_in,
+    hidden_out,
+    hidden_in,
+    back_out,
+    back_in,
+    last_out,
+    last_in,
+    load_sem,
+    send_sem,
+    recv_sem,
+    pair_sem,
+):
+    sec = lax.axis_index("sec")
+    dev = lax.axis_index("dev")
+    rows_here, kv_heads, span, head_dim = keys.shape
+    group = query_rows.shape[1] // rows_here
+    rows = n_dev * rows_here
+    cols = out_proj.shape[0]
+    kv_width = group * head_dim
+
+    loads = [
+        pltpu.make_async_copy(source, target, load_sem.at[i])
+        for i, (source, target) in enumerate(
+            (
+                (keys_hbm, keys),
+                (values_hbm, values),
+                (out_proj_hbm, out_proj),
+                (gate_hbm.at[0], gate_w),
+                (up_hbm.at[0], up_w),
+                (down_hbm.at[0], down_w),
+            )
+        )
+    ]
+    for load in loads:
+        load.start()
+
+    barrier = pltpu.get_barrier_semaphore()
+    pair = {"sec": 1 - sec}
+    pl.semaphore_signal(barrier, inc=1, device_id=pair, device_id_type=MESH)
+
+    @pl.loop(1, n_dev)
+    def _(step):
+        peer = lax.rem(dev + step, n_dev)
+        pl.semaphore_signal(barrier, inc=1, device_id={"dev": peer}, device_id_type=MESH)
+
+    def exchange(phase, source_of, target_of):
+        @pl.loop(1, n_dev)
+        def _(step):
+            peer = lax.rem(dev + step, n_dev)
+            pltpu.make_async_remote_copy(
+                src_ref=source_of(peer),
+                dst_ref=target_of(dev),
+                send_sem=send_sem.at[phase, peer],
+                recv_sem=recv_sem.at[phase, dev],
+                device_id={"dev": peer},
+                device_id_type=MESH,
+            ).start()
+
+    def settle(phase, source_of, target_of, sent):
+        @pl.loop(1, n_dev)
+        def _(step):
+            peer = lax.rem(dev + step, n_dev)
+            copy = pltpu.make_async_remote_copy(
+                src_ref=source_of(peer),
+                dst_ref=target_of(peer),
+                send_sem=send_sem.at[phase, peer],
+                recv_sem=recv_sem.at[phase, peer],
+                device_id={"dev": peer},
+                device_id_type=MESH,
+            )
+            if sent:
+                copy.wait_send()
+            else:
+                copy.wait_recv()
+
+    def across(phase, source, target):
+        copy = pltpu.make_async_remote_copy(
+            src_ref=source,
+            dst_ref=target,
+            send_sem=pair_sem.at[phase, 0],
+            recv_sem=pair_sem.at[phase, 1],
+            device_id=pair,
+            device_id_type=MESH,
+        )
+        copy.start()
+        return copy
+
+    wide_queries = queries[...].astype(jnp.float32)
+    for row in range(rows_here):
+        for kv in range(kv_heads):
+            for g in range(group):
+                start = (kv * group + g) * head_dim
+                query_rows[kv, row * group + g : row * group + g + 1, :] = wide_queries[
+                    row : row + 1, start : start + head_dim
+                ]
+    loads[0].wait()
+    loads[1].wait()
+    position = lax.broadcasted_iota(jnp.int32, (group, span), 1)
+    for row in range(rows_here):
+        live = position < lengths[row]
+        for kv in range(kv_heads):
+            query = query_rows[kv, row * group : (row + 1) * group, :].astype(jnp.bfloat16)
+            scores = times_transpose(query, keys[row, kv]) * (1.0 / math.sqrt(head_dim))
+            scores = jnp.where(live, scores, -jnp.inf)
+            raised = jnp.exp(scores - jnp.max(scores, axis=1, keepdims=True))
+            probs = (raised / jnp.sum(raised, axis=1, keepdims=True)).astype(jnp.bfloat16)
+            found = jnp.dot(probs, values[row, kv], preferred_element_type=jnp.float32)
+            found = found.astype(jnp.bfloat16)
+            heads_out[kv * rows_here + row] = found
+            heads_in[dev, kv * rows_here + row] = found
+
+    pl.semaphore_wait(barrier, n_dev)
+    exchange(0, lambda peer: heads_out, lambda peer: heads_in.at[peer])
+
+    named = jnp.int32(0)
+    for e in range(owners.shape[0]):
+        named = named + jnp.where(owners[e] == dev, jnp.int32(e), jnp.int32(0))
+    weight = jnp.sum(
+        jnp.where(expert_ids[...] == named, gate_weights[...], 0.0), axis=1, keepdims=True
+    )
+
+    settle(0, lambda peer: heads_out, lambda peer: heads_in.at[peer], False)
+    loads[2].wait()
+    part = jnp.zeros((rows, cols), jnp.float32)
+    for kv in range(kv_heads):
+        for d in range(n_dev):
+            for row in range(rows_here):
+                place = (d * rows_here + row) * group
+                heads_wide[place : place + group, :] = heads_in[d, kv * rows_here + row].astype(
+                    jnp.float32
+                )
+        features = jnp.concatenate(
+            [heads_wide[pl.ds(g, rows, stride=group), :] for g in range(group)], axis=1
+        ).astype(jnp.bfloat16)
+        part = part + times_transpose(
+            features, out_proj[:, kv * kv_width : (kv + 1) * kv_width]
+        )
+    part_out[...] = part
+    swap = across(0, part_out, part_in)
+    swap.wait_recv()
+    base = residual[...].astype(jnp.float32) + (part + part_in[...])
+    hidden = base.astype(jnp.bfloat16)
+    hidden_out[...] = hidden
+    hidden_in[dev] = hidden
+    exchange(1, lambda peer: hidden_out, lambda peer: hidden_in.at[peer])
+    settle(1, lambda peer: hidden_out, lambda peer: hidden_in.at[peer], False)
+
+    arrived = jnp.concatenate([hidden_in[d] for d in range(n_dev)], axis=1).astype(jnp.float32)
+    square_mean = jnp.mean(arrived * arrived, axis=1, keepdims=True)
+    normed = (
+        arrived * lax.rsqrt(square_mean + epsilon) * norm_gain[...].astype(jnp.float32)
+    ).astype(jnp.bfloat16)
+    loads[3].wait()
+    loads[4].wait()
+    gate_act = times_transpose(normed, gate_w[...])
+    up_act = times_transpose(normed, up_w[...])
+    act = (gate_act * (1.0 / (1.0 + jnp.exp(-gate_act))) * up_act).astype(jnp.bfloat16)
+    loads[5].wait()
+    for d in range(n_dev):
+        made = jnp.dot(
+            act, down_w[:, d * cols : (d + 1) * cols], preferred_element_type=jnp.float32
+        )
+        back_out[d] = (made * weight).astype(jnp.bfloat16)
+    exchange(2, lambda peer: back_out.at[peer], lambda peer: back_in.at[peer])
+    back_in[dev] = back_out[dev]
+    settle(2, lambda peer: back_out.at[peer], lambda peer: back_in.at[peer], False)
+    moe = back_in[0].astype(jnp.float32)
+    for d in range(1, n_dev):
+        moe = moe + back_in[d].astype(jnp.float32)
+    last_out[...] = moe
+    last = across(1, last_out, last_in)
+    last.wait_recv()
+    output[...] = (base + (moe + last_in[...])).astype(jnp.bfloat16)
+
+    settle(0, lambda peer: heads_out, lambda peer: heads_in.at[peer], True)
+    settle(1, lambda peer: hidden_out, lambda peer: hidden_in.at[peer], True)
+    settle(2, lambda peer: back_out.at[peer], lambda peer: back_in.at[peer], True)
+    swap.wait_send()
+    last.wait_send()
+
+
+def fused(
+    n_dev,
+    queries,
+    cache_keys,
+    cache_values,
+    lengths,
+    out_proj,
+    residual,
+    norm_gain,
+    expert_ids,
+    gate_weights,
+    owners,
+    gate_proj,
+    up_proj,
+    down_proj,
+):
+    rows_here, kv_heads, span, head_dim = cache_keys.shape
+    cols = out_proj.shape[0]
+    rows, width = residual.shape[0], norm_gain.shape[0]
+    group = queries.shape[1] // (kv_heads * head_dim)
+    units = gate_proj.shape[1]
+    vmem = pl.BlockSpec(memory_space=pltpu.VMEM)
+    smem = pl.BlockSpec(memory_space=pltpu.SMEM)
+    whole = pl.BlockSpec(memory_space=pl.ANY)
+    wide, narrow = jnp.float32, jnp.bfloat16
+    blocks = rows_here * kv_heads
+    return pl.pallas_call(
+        functools.partial(fused_kernel, n_dev),
+        out_shape=jax.ShapeDtypeStruct((rows, cols), narrow),
+        in_specs=[vmem, smem, vmem, vmem, vmem, vmem, smem] + [whole] * 6,
+        out_specs=vmem,
+        scratch_shapes=[
+            pltpu.VMEM(cache_keys.shape, narrow),
+            pltpu.VMEM(cache_values.shape, narrow),
+            pltpu.VMEM(out_proj.shape, narrow),
+            pltpu.VMEM((units, width), narrow),
+            pltpu.VMEM((units, width), narrow),
+            pltpu.VMEM((units, width), narrow),
+            pltpu.VMEM((kv_heads, rows_here * group, head_dim), wide),
+            pltpu.VMEM((blocks, group, head_dim), narrow),
+            pltpu.VMEM((n_dev, blocks, group, head_dim), narrow),
+            pltpu.VMEM((rows * group, head_dim), wide),
+            pltpu.VMEM((rows, cols), wide),
+            pltpu.VMEM((rows, cols), wide),
+            pltpu.VMEM((rows, cols), narrow),
+            pltpu.VMEM((n_dev, rows, cols), narrow),
+            pltpu.VMEM((n_dev, rows, cols), narrow),
+            pltpu.VMEM((n_dev, rows, cols), narrow),
+            pltpu.VMEM((rows, cols), wide),
+            pltpu.VMEM((rows, cols), wide),
+            pltpu.SemaphoreType.DMA((6,)),
+            pltpu.SemaphoreType.DMA((3, n_dev)),
+            pltpu.SemaphoreType.DMA((3, n_dev)),
+            pltpu.SemaphoreType.DMA((2, 2)),
+        ],
+        compiler_params=pltpu.CompilerParams(
+            collective_id=0, has_side_effects=True, vmem_limit_bytes=48 * 1024 * 1024
+        ),
+        cost_estimate=pl.CostEstimate(
+            flops=2 * rows * width * (width + 3 * units),
+            bytes_accessed=2 * width * (width + 3 * units),
+            transcendentals=0,
+        ),
+    )(
+        queries,
+        lengths,
+        residual,
+        norm_gain.reshape(1, width),
+        expert_ids,
+        gate_weights,
+        owners,
+        cache_keys,
+        cache_values,
+        out_proj,
+        gate_proj,
+        up_proj,
+        down_proj,
+    )
+
+
+def tiles_whole(mesh, operands):
+    queries, cache_keys, _, _, out_proj, residual = operands[:6]
+    owners, gate_proj = operands[9], operands[10]
+    group = queries.shape[1] // (cache_keys.shape[1] * cache_keys.shape[3])
+    return (
+        mesh.shape["sec"] == 2
+        and owners.shape[0] == mesh.shape["dev"]
+        and gate_proj.shape[0] == 1
+        and group % 16 == 0
+        and cache_keys.shape[3] % 128 == 0
+        and cache_keys.shape[2] % 128 == 0
+        and residual.shape[0] % 16 == 0
+        and out_proj.shape[0] % 128 == 0
+        and gate_proj.shape[1] % 128 == 0
+    )
+
+
 def solution(mesh):
     in_specs = (
         P("dev", "sec"),
@@ -139,4 +448,10 @@
         P("dev", "sec", None),
     )
     out_specs = P(None, "dev")
-    return jax.shard_map(shards, mesh=mesh, in_specs=in_specs, out_specs=out_specs, check_vma=False)
+
+    def chosen(*operands):
+        if tiles_whole(mesh, operands):
+            return fused(mesh.shape["dev"], *operands)
+        return shards(*operands)
+
+    return jax.shard_map(chosen, mesh=mesh, in_specs=in_specs, out_specs=out_specs, check_vma=False)

time: 132 us -> 47.2 us (0.36)
  blocking collectives: 54.3 us -> 0 us
  Pallas kernels: 0 us -> 37 us
  other arithmetic: 28.1 us -> 0 us
  matrix products: 13.6 us -> 0 us
  local copies, waits for them, and re-layouts: 21.2 us -> 9.26 us
  waiting for transfers between devices: 9.66 us -> 0 us
  starting transfers between devices: 3.53 us -> 0 us
    pallas_call x0 -> x1, Pallas kernels: none -> 37 us  [fused(): pl.pallas_call(functools.partial(fused_kernel, n_dev), out_shape=jax.Shap...]
    all_gather x1 -> x0, blocking collectives: 25.2 us -> none  [shards(): lax.all_gather(head_out, 'dev', axis=0, tiled=True)]
    unnamed x2 -> x0, other arithmetic: 24.6 us -> none
    psum x2 -> x0, blocking collectives: 15.7 us -> none  [the longest x1 8.35 us: shards(): attention_out = lax.psum(attention_part, 'sec')]
    dot_general x7 -> x0, matrix products: 13.6 us -> none  [the longest x2 5.23 us: times_transpose(): lax.dot_general(left, right, (((1,), (1,)), ((), ())), preferred_element_...]
    all_to_all x1 -> x0, blocking collectives: 13.3 us -> none  [shards(): lax.all_to_all(weighted.reshape(1, capacity, weighted.shape[1]), 'dev', s...]
    all_to_all x1 -> x0, waiting for transfers between devices: 9.66 us -> none  [shards(): lax.all_to_all(outbound, 'dev', split_axis=0, concat_axis=2, tiled=True)]
    all_to_all x3 -> x0, local copies, waits for them, and re-layouts: 4.57 us -> none  [shards(): lax.all_to_all(weighted.reshape(1, capacity, weighted.shape[1]), 'dev', s...]
  transfers between devices with their start and end apart: 1 -> 0, of which waited for: 1 -> 0; matrix products, arithmetic and copies ran while one was open for 0% -> 0% of each run, Pallas kernels for 0% -> 0%
where the time goes in v1:
time: 47.2 us; the launch traced here: 46.3 us
  Pallas kernels  37 us (78%)
  local copies, waits for them, and re-layouts  9.26 us (20%)
    pallas_call x1, Pallas kernels, fused(): pl.pallas_call(functools.partial(fused_kernel, n_dev), out_shape=jax.Shap...  37 us
    unnamed x17, local copies, waits for them, and re-layouts  8.55 us

profile of v1, /device:TPU:0, one launch (start us, length us, event | category | flops | bytes accessed | tf_op | source)
XLA Modules:
  0.0 46.3 jit_solution(1376092365901203860)
XLA Ops:
  0.0 0.7 %reshape.3.norm_gain = bf16[1,4096]{1,0:T(2,128)(2,1)S(1)} reshape(bf16[4096]{0:T(1024)(128)(2,1)} %param.19) | data formatting | bytes 16384 | tf_op jit(solution)/shard_map/reshape | solution.py:404
  0.7 0.8 %copy.14.expert_ids = s32[32,8]{1,0:T(8,128)S(1)} copy(s32[32,8]{0,1:T(8,128)} %param.20) | data formatting | bytes 2048 | tf_op args[7]
  1.5 0.8 %copy.15.gate_weights = f32[32,8]{1,0:T(8,128)S(1)} copy(f32[32,8]{0,1:T(8,128)} %param.21) | data formatting | bytes 2048 | tf_op args[8]
  2.2 0.0 copy-start
  2.2 1.6 %copy-done = bf16[256,4096]{1,0:T(8,128)(2,1)S(1)} copy-done((bf16[256,4096]{1,0:T(8,128)(2,1)S(1)}, bf16[256,4096]{1,0:T(8,128)(2,1)}, u32[]{:S(2)}) %copy-start) | copy-done | bytes 2097176
  3.8 0.0 copy-start.1
  3.8 1.0 %copy-done.1 = bf16[2,2,512,128]{3,2,1,0:T(8,128)(2,1)S(1)} copy-done((bf16[2,2,512,128]{3,2,1,0:T(8,128)(2,1)S(1)}, bf16[2,2,512,128]{3,2,1,0:T(8,128)(2,1)}, u32[]{:S(2)}) %copy-start.1) | copy-done | bytes 524312
  4.9 0.0 copy-start.2
  4.9 1.0 %copy-done.2 = bf16[2,2,512,128]{3,2,1,0:T(8,128)(2,1)S(1)} copy-done((bf16[2,2,512,128]{3,2,1,0:T(8,128)(2,1)S(1)}, bf16[2,2,512,128]{3,2,1,0:T(8,128)(2,1)}, u32[]{:S(2)}) %copy-start.2) | copy-done | bytes 524312
  5.9 0.0 copy-start.3
  5.9 0.7 %copy-done.3 = bf16[2,4096]{1,0:T(2,128)(2,1)S(1)} copy-done((bf16[2,4096]{1,0:T(2,128)(2,1)S(1)}, bf16[2,4096]{1,0:T(2,128)(2,1)}, u32[]{:S(2)}) %copy-start.3) | copy-done | bytes 16408
  6.6 0.0 copy-start.4
  6.6 0.7 %copy-done.4 = bf16[32,256]{1,0:T(8,128)(2,1)S(1)} copy-done((bf16[32,256]{1,0:T(8,128)(2,1)S(1)}, bf16[32,256]{1,0:T(8,128)(2,1)}, u32[]{:S(2)}) %copy-start.4) | copy-done | bytes 16408
  7.3 0.0 copy-start.5
  7.4 0.7 %copy-done.5 = s32[2]{0:T(128)S(1)} copy-done((s32[2]{0:T(128)S(1)}, s32[2]{0:T(128)}, u32[]{:S(2)}) %copy-start.5) | copy-done | bytes 32
  8.0 0.0 copy-start.6
  8.0 0.7 %copy-done.6 = s32[16]{0:T(128)S(1)} copy-done((s32[16]{0:T(128)S(1)}, s32[16]{0:T(128)}, u32[]{:S(2)}) %copy-start.6) | copy-done | bytes 88
  8.7 37.0 %shard_map.127 = bf16[32,256]{1,0:T(8,128)(2,1)S(1)} custom-call(bf16[2,4096]{1,0:T(2,128)(2,1)S(1)} %copy-done.3, s32[2]{0:T(128)S(1)} %copy-done.5, bf16[32,256]{1,0:T(8,128)(2,1)S(1)} %copy-done.4, bf16[1,4096]{1,0:T(2,128)(2,1)S(1)} %reshape.3.norm_gain, s32[32,8]{1,0:T(8,128)S(1)} %copy.14.expert_ids, f32[32,8]{1,0:T(8,128)S(1)} %copy.15.gate_weights, ...), custom_call_target="tpu_custom_call" | custom-call | flops 1375731712 | bytes 42991616 | tf_op jit(solution)/shard_map/pallas_call | solution.py:363
  45.7 0.6 %copy.17 = bf16[32,256]{1,0:T(8,128)(2,1)} copy(bf16[32,256]{1,0:T(8,128)(2,1)S(1)} %shard_map.127) | data formatting | bytes 32768
Async XLA Ops:
  2.2 1.6 %copy-start = (bf16[256,4096]{1,0:T(8,128)(2,1)S(1)}, bf16[256,4096]{1,0:T(8,128)(2,1)}, u32[]{:S(2)}) copy-start(bf16[256,4096]{1,0:T(8,128)(2,1)} %out_proj_hbm.1) | copy-start | bytes 6291460
  3.8 1.0 %copy-start.1 = (bf16[2,2,512,128]{3,2,1,0:T(8,128)(2,1)S(1)}, bf16[2,2,512,128]{3,2,1,0:T(8,128)(2,1)}, u32[]{:S(2)}) copy-start(bf16[2,2,512,128]{3,2,1,0:T(8,128)(2,1)} %keys_hbm.1) | copy-start | bytes 1572868
  4.9 1.0 %copy-start.2 = (bf16[2,2,512,128]{3,2,1,0:T(8,128)(2,1)S(1)}, bf16[2,2,512,128]{3,2,1,0:T(8,128)(2,1)}, u32[]{:S(2)}) copy-start(bf16[2,2,512,128]{3,2,1,0:T(8,128)(2,1)} %values_hbm.1) | copy-start | bytes 1572868
  5.9 0.7 %copy-start.3 = (bf16[2,4096]{1,0:T(2,128)(2,1)S(1)}, bf16[2,4096]{1,0:T(2,128)(2,1)}, u32[]{:S(2)}) copy-start(bf16[2,4096]{1,0:T(2,128)(2,1)} %queries.1) | copy-start | bytes 49156
  6.6 0.7 %copy-start.4 = (bf16[32,256]{1,0:T(8,128)(2,1)S(1)}, bf16[32,256]{1,0:T(8,128)(2,1)}, u32[]{:S(2)}) copy-start(bf16[32,256]{1,0:T(8,128)(2,1)} %residual.1) | copy-start | bytes 49156
  7.3 0.7 %copy-start.5 = (s32[2]{0:T(128)S(1)}, s32[2]{0:T(128)}, u32[]{:S(2)}) copy-start(s32[2]{0:T(128)} %lengths.1) | copy-start | bytes 28
  8.0 0.7 %copy-start.6 = (s32[16]{0:T(128)S(1)}, s32[16]{0:T(128)}, u32[]{:S(2)}) copy-start(s32[16]{0:T(128)} %owners.1) | copy-start | bytes 196

commit v2 on v1

v2 whole, which is shorter than its diff:
```python
import functools
import math

import jax
import jax.numpy as jnp
from jax import lax
from jax.experimental import pallas as pl
from jax.experimental.pallas import tpu as pltpu
from jax.sharding import PartitionSpec as P

epsilon = 1e-05
MESH = pl.DeviceIdType.MESH


def slot_targets(expert_ids, owners, capacity):
    experts = owners.shape[0]
    flat_ids = expert_ids.reshape(-1)
    one_hot = (flat_ids[:, None] == jnp.arange(experts, dtype=jnp.int32)[None, :]).astype(jnp.int32)
    before = jnp.cumsum(one_hot, axis=0) - one_hot
    position = jnp.sum(before * one_hot, axis=1)
    holder = jnp.sum(one_hot * owners[None, :], axis=1)
    return (holder * capacity + position).reshape(expert_ids.shape)


def routing_tables(expert_ids, gate_weights, owners, capacity):
    target = slot_targets(expert_ids, owners, capacity)
    places = jnp.arange(owners.shape[0] * capacity, dtype=jnp.int32)
    matched = target[None, :, :] == places[:, None, None]
    sending = jnp.any(matched, axis=2)
    weighting = jnp.sum(
        jnp.where(matched, gate_weights[None, :, :], jnp.zeros_like(gate_weights)[None, :, :]),
        axis=2,
    )
    return (sending, weighting)


def times_transpose(left, right):
    return lax.dot_general(
        left, right, (((1,), (1,)), ((), ())), preferred_element_type=jnp.float32
    )


def attend(queries, cache_keys, cache_values, lengths):
    rows, kv_heads, key_span, head_dim = cache_keys.shape
    group_size = queries.shape[1] // (kv_heads * head_dim)
    grouped = queries.reshape(rows, kv_heads, group_size, head_dim)
    scores = jnp.einsum(
        "rkgd,rktd->rkgt", grouped, cache_keys, preferred_element_type=jnp.float32
    ) / math.sqrt(head_dim)
    live_mask = (
        jnp.arange(key_span, dtype=jnp.int32)[None, None, None, :] < lengths[:, None, None, None]
    )
    scores = jnp.where(live_mask, scores, -jnp.inf)
    row_top = jnp.max(scores, axis=-1, keepdims=True)
    raised = jnp.exp(scores - row_top)
    soft_weight = (raised / jnp.sum(raised, axis=-1, keepdims=True)).astype(jnp.bfloat16)
    head_out = jnp.einsum(
        "rkgt,rktd->rkgd", soft_weight, cache_values, preferred_element_type=jnp.float32
    )
    return head_out.astype(jnp.bfloat16).reshape(rows, -1)


def root_norm(arrived, norm_gain):
    square_mean = jnp.mean(arrived * arrived, axis=-1, keepdims=True)
    return (arrived * lax.rsqrt(square_mean + epsilon) * norm_gain.astype(jnp.float32)).astype(
        jnp.bfloat16
    )


def expert_ffn(normed, gate_w, up_w, down_w):
    gate_act = times_transpose(normed, gate_w)
    up_act = times_transpose(normed, up_w)
    hidden = (jax.nn.silu(gate_act) * up_act).astype(jnp.bfloat16)
    return jnp.dot(hidden, down_w, preferred_element_type=jnp.float32)


def shards(
    queries,
    cache_keys,
    cache_values,
    lengths,
    out_proj,
    residual,
    norm_gain,
    expert_ids,
    gate_weights,
    owners,
    gate_proj,
    up_proj,
    down_proj,
):
    head_out = attend(queries, cache_keys, cache_values, lengths)
    attention_part = times_transpose(lax.all_gather(head_out, "dev", axis=0, tiled=True), out_proj)
    rows_all, top_count = expert_ids.shape
    experts = owners.shape[0]
    capacity = min(rows_all, 3 * top_count * rows_all // experts)
    col_count = out_proj.shape[0]
    sending, weighting = routing_tables(expert_ids, gate_weights, owners, capacity)
    residual_wide = residual.astype(jnp.float32)
    attention_out = lax.psum(attention_part, "sec")
    hidden_in = (residual_wide + attention_out).astype(jnp.bfloat16)
    outbound = jnp.dot(sending.astype(jnp.bfloat16), hidden_in, preferred_element_type=jnp.float32)
    outbound = outbound.astype(jnp.bfloat16).reshape(experts, capacity, col_count)
    inbound = lax.all_to_all(outbound, "dev", split_axis=0, concat_axis=2, tiled=True)
    arrived = inbound[0].astype(jnp.float32)
    normed = root_norm(arrived, norm_gain)
    expert_out = expert_ffn(normed, gate_proj[0], up_proj[0], down_proj[0])
    place_weight = jnp.sum(weighting, axis=1)
    own_weight = lax.dynamic_slice_in_dim(
        place_weight, lax.axis_index("dev") * capacity, capacity, 0
    )
    weighted = (expert_out * own_weight[:, None]).astype(jnp.bfloat16)
    returned = lax.all_to_all(
        weighted.reshape(1, capacity, weighted.shape[1]),
        "dev",
        split_axis=2,
        concat_axis=0,
        tiled=True,
    )
    moe = jnp.dot(
        sending.T.astype(jnp.bfloat16),
        returned.reshape(-1, col_count),
        preferred_element_type=jnp.float32,
    )
    summed = lax.psum(moe, "sec")
    return (residual_wide + attention_out + summed).astype(jnp.bfloat16)
VMEM_LIMIT = 64 * 1024 * 1024 - 64 * 1024


def fused_kernel(
    n_dev,
    queries_hbm,
    lengths_hbm,
    residual_hbm,
    gain_hbm,
    ids_hbm,
    router_hbm,
    owners_hbm,
    keys_hbm,
    values_hbm,
    out_proj_hbm,
    gate_hbm,
    up_hbm,
    down_hbm,
    output,
    queries,
    lengths,
    residual,
    gain,
    ids,
    router,
    owners,
    keys,
    values,
    out_proj,
    rising,
    down_w,
    query_rows,
    heads_in,
    heads_wide,
    part_out,
    part_in,
    hidden_in,
    cross_out,
    cross_in,
    back_out,
    back_in,
    last_out,
    last_in,
    load_sem,
    send_sem,
    recv_sem,
    pass_sem,
    back_send_sem,
    back_recv_sem,
    pair_sem,
):
    sec = lax.axis_index("sec")
    dev = lax.axis_index("dev")
    chip, core = lax.div(dev, 2), lax.rem(dev, 2)
    chips = n_dev // 2
    rows_here, kv_heads, span, head_dim = keys.shape
    group = query_rows.shape[1] // rows_here
    rows = n_dev * rows_here
    cols = out_proj.shape[0]
    units = down_w.shape[0]
    kv_width = group * head_dim

    def flipped(k):
        bit, place = 1, 0
        while bit < chips:
            place = place + lax.rem(lax.div(chip, bit) + (k // bit) % 2, 2) * bit
            bit *= 2
        return place

    chip_of = [flipped(k) for k in range(chips)]
    twin = 2 * chip + 1 - core
    to_twin = {"dev": twin}
    across = {"sec": 1 - sec}
    same = [2 * chip_of[k] + core for k in range(chips)]
    other = [2 * chip_of[k] + 1 - core for k in range(chips)]

    pairs = (
        (queries_hbm, queries),
        (keys_hbm, keys),
        (values_hbm, values),
        (lengths_hbm, lengths),
        (out_proj_hbm, out_proj),
        (residual_hbm, residual),
        (gain_hbm, gain),
        (ids_hbm, ids),
        (router_hbm, router),
        (owners_hbm, owners),
        (gate_hbm.at[0], rising.at[pl.ds(0, units)]),
        (up_hbm.at[0], rising.at[pl.ds(units, units)]),
        (down_hbm.at[0], down_w),
    )
    loads = [
        pltpu.make_async_copy(source, target, load_sem.at[i])
        for i, (source, target) in enumerate(pairs)
    ]
    for load in loads:
        load.start()

    barrier = pltpu.get_barrier_semaphore()
    for place in [across, to_twin] + [{"dev": same[k]} for k in range(1, chips)]:
        pl.semaphore_signal(barrier, inc=1, device_id=place, device_id_type=MESH)

    def remote(source, target, sent, received, place):
        return pltpu.make_async_remote_copy(
            src_ref=source,
            dst_ref=target,
            send_sem=sent,
            recv_sem=received,
            device_id=place,
            device_id_type=MESH,
        )

    def landed(phase, buffer, index):
        remote(
            buffer.at[index], buffer.at[index], send_sem.at[phase, 0],
            recv_sem.at[phase, index], to_twin,
        ).wait_recv()

    def gather_start(phase, buffer):
        copies = []
        for k in reversed(range(chips)):
            place = {"dev": same[k]} if k else to_twin
            copies.append(
                remote(
                    buffer.at[dev], buffer.at[dev], send_sem.at[phase, k],
                    recv_sem.at[phase, dev], place,
                )
            )
            copies[-1].start()
        return copies

    def gather_pass(phase, buffer, k):
        landed(phase, buffer, same[k])
        copy = remote(
            buffer.at[same[k]], buffer.at[same[k]], pass_sem.at[phase, k],
            recv_sem.at[phase, same[k]], to_twin,
        )
        copy.start()
        return copy

    loads[0].wait()
    wide_queries = queries[...].astype(jnp.float32)
    for row in range(rows_here):
        for kv in range(kv_heads):
            for g in range(group):
                start = (kv * group + g) * head_dim
                query_rows[kv, row * group + g : row * group + g + 1, :] = wide_queries[
                    row : row + 1, start : start + head_dim
                ]
    loads[1].wait()
    loads[3].wait()
    position = lax.broadcasted_iota(jnp.int32, (group, span), 1)
    scores = []
    for kv in range(kv_heads):
        for row in range(rows_here):
            query = query_rows[kv, row * group : (row + 1) * group, :].astype(jnp.bfloat16)
            found = times_transpose(query, keys[row, kv]) * (1.0 / math.sqrt(head_dim))
            scores.append(jnp.where(position < lengths[row], found, -jnp.inf))
    scores = jnp.concatenate(scores, axis=0)
    raised = jnp.exp(scores - jnp.max(scores, axis=1, keepdims=True))
    probs = (raised / jnp.sum(raised, axis=1, keepdims=True)).astype(jnp.bfloat16)
    loads[2].wait()
    for kv in range(kv_heads):
        for row in range(rows_here):
            block = kv * rows_here + row
            found = jnp.dot(
                probs[block * group : (block + 1) * group],
                values[row, kv],
                preferred_element_type=jnp.float32,
            )
            heads_in[dev, block] = found.astype(jnp.bfloat16)

    pl.semaphore_wait(barrier, chips + 1)
    sends = gather_start(0, heads_in)

    for i in (5, 6, 7, 8, 9):
        loads[i].wait()
    named = jnp.int32(0)
    for e in range(owners.shape[0]):
        named = named + jnp.where(owners[e] == dev, jnp.int32(e), jnp.int32(0))
    lying = jnp.sum(jnp.where(ids[...] == named, router[...], 0.0), axis=0, keepdims=True)
    square = (rows, rows)
    diagonal = lax.broadcasted_iota(jnp.int32, square, 0) == lax.broadcasted_iota(
        jnp.int32, square, 1
    )
    weight = jnp.sum(
        jnp.where(diagonal, jnp.broadcast_to(lying, square), 0.0), axis=1, keepdims=True
    )

    for k in range(1, chips):
        sends.append(gather_pass(0, heads_in, k))
    for k in range(chips):
        landed(0, heads_in, other[k])
    loads[4].wait()
    for kv in range(kv_heads):
        for d in range(n_dev):
            for row in range(rows_here):
                place = (d * rows_here + row) * group
                heads_wide[kv, place : place + group, :] = heads_in[
                    d, kv * rows_here + row
                ].astype(jnp.float32)
    features = jnp.concatenate(
        [
            heads_wide[kv, pl.ds(g, rows, stride=group), :]
            for kv in range(kv_heads)
            for g in range(group)
        ],
        axis=1,
    ).astype(jnp.bfloat16)
    part = times_transpose(features, out_proj[...])
    part_out[...] = part
    swap = remote(part_out, part_in, pair_sem.at[0, 0], pair_sem.at[0, 1], across)
    swap.start()
    sends.append(swap)
    swap.wait_recv()
    base = residual[...].astype(jnp.float32) + (part + part_in[...])
    hidden_in[dev] = base.astype(jnp.bfloat16)
    sends += gather_start(1, hidden_in)

    loads[10].wait()
    loads[11].wait()
    squares = jnp.zeros((rows, cols), jnp.float32)
    raising = jnp.zeros((rows, 2 * units), jnp.float32)

    def take(index, squares, raising):
        start = pl.multiple_of(index * cols, cols)
        block = hidden_in[index].astype(jnp.float32)
        scaled = (block * gain[pl.ds(start, cols)].astype(jnp.float32).reshape(1, cols)).astype(jnp.bfloat16)
        return (
            squares + block * block,
            raising + times_transpose(scaled, rising[:, pl.ds(start, cols)]),
        )

    squares, raising = take(dev, squares, raising)
    for k in range(chips):
        if k:
            sends.append(gather_pass(1, hidden_in, k))
            squares, raising = take(same[k], squares, raising)
        landed(1, hidden_in, other[k])
        squares, raising = take(other[k], squares, raising)
    square_mean = jnp.sum(squares, axis=1, keepdims=True) / (n_dev * cols)
    raising = raising * lax.rsqrt(square_mean + epsilon)
    gate_act, up_act = raising[:, :units], raising[:, units:]
    act = (gate_act * (1.0 / (1.0 + jnp.exp(-gate_act))) * up_act).astype(jnp.bfloat16)

    def lowered(index):
        start = pl.multiple_of(index * cols, cols)
        made = jnp.dot(act, down_w[:, pl.ds(start, cols)], preferred_element_type=jnp.float32)
        return made * weight

    loads[12].wait()
    crossing = {}
    for k in reversed(range(chips)):
        cross_out[k] = lowered(other[k]).astype(jnp.bfloat16)
        crossing[k] = remote(
            cross_out.at[k], cross_in.at[k], back_send_sem.at[0, k], back_recv_sem.at[0, k], to_twin
        )
        crossing[k].start()
        sends.append(crossing[k])
    backs = {}
    for k in reversed(range(chips)):
        made = lowered(same[k])
        crossing[k].wait_recv()
        made = made + cross_in[k].astype(jnp.float32)
        if k == 0:
            moe = made
            continue
        back_out[k] = made.astype(jnp.bfloat16)
        backs[k] = remote(
            back_out.at[k], back_in.at[k], back_send_sem.at[1, k], back_recv_sem.at[1, k],
            {"dev": same[k]},
        )
        backs[k].start()
        sends.append(backs[k])
    for k in range(1, chips):
        backs[k].wait_recv()
        moe = moe + back_in[k].astype(jnp.float32)
    last_out[...] = moe
    last = remote(last_out, last_in, pair_sem.at[1, 0], pair_sem.at[1, 1], across)
    last.start()
    sends.append(last)
    last.wait_recv()
    output[...] = (base + (moe + last_in[...])).astype(jnp.bfloat16)
    for copy in sends:
        copy.wait_send()


def fused(
    n_dev,
    queries,
    cache_keys,
    cache_values,
    lengths,
    out_proj,
    residual,
    norm_gain,
    expert_ids,
    gate_weights,
    owners,
    gate_proj,
    up_proj,
    down_proj,
):
    rows_here, kv_heads, span, head_dim = cache_keys.shape
    cols = out_proj.shape[0]
    rows, width = residual.shape[0], norm_gain.shape[0]
    group = queries.shape[1] // (kv_heads * head_dim)
    units = gate_proj.shape[1]
    chips = n_dev // 2
    whole = pl.BlockSpec(memory_space=pltpu.HBM)
    wide, narrow = jnp.float32, jnp.bfloat16
    blocks = rows_here * kv_heads
    gain = norm_gain
    return pl.pallas_call(
        functools.partial(fused_kernel, n_dev),
        out_shape=jax.ShapeDtypeStruct((rows, cols), narrow),
        in_specs=[whole] * 13,
        out_specs=pl.BlockSpec(memory_space=pltpu.VMEM),
        scratch_shapes=[
            pltpu.VMEM(queries.shape, narrow),
            pltpu.SMEM(lengths.shape, jnp.int32),
            pltpu.VMEM(residual.shape, narrow),
            pltpu.VMEM(gain.shape, narrow),
            pltpu.VMEM(expert_ids.shape[::-1], jnp.int32),
            pltpu.VMEM(gate_weights.shape[::-1], wide),
            pltpu.SMEM(owners.shape, jnp.int32),
            pltpu.VMEM(cache_keys.shape, narrow),
            pltpu.VMEM(cache_values.shape, narrow),
            pltpu.VMEM(out_proj.shape, narrow),
            pltpu.VMEM((2 * units, width), narrow),
            pltpu.VMEM((units, width), narrow),
            pltpu.VMEM((kv_heads, rows_here * group, head_dim), wide),
            pltpu.VMEM((n_dev, blocks, group, head_dim), narrow),
            pltpu.VMEM((kv_heads, rows * group, head_dim), wide),
            pltpu.VMEM((rows, cols), wide),
            pltpu.VMEM((rows, cols), wide),
            pltpu.VMEM((n_dev, rows, cols), narrow),
            pltpu.VMEM((chips, rows, cols), narrow),
            pltpu.VMEM((chips, rows, cols), narrow),
            pltpu.VMEM((chips, rows, cols), narrow),
            pltpu.VMEM((chips, rows, cols), narrow),
            pltpu.VMEM((rows, cols), wide),
            pltpu.VMEM((rows, cols), wide),
            pltpu.SemaphoreType.DMA((13,)),
            pltpu.SemaphoreType.DMA((2, chips)),
            pltpu.SemaphoreType.DMA((2, n_dev)),
            pltpu.SemaphoreType.DMA((2, chips)),
            pltpu.SemaphoreType.DMA((2, chips)),
            pltpu.SemaphoreType.DMA((2, chips)),
            pltpu.SemaphoreType.DMA((2, 2)),
        ],
        compiler_params=pltpu.CompilerParams(
            collective_id=0, has_side_effects=True, vmem_limit_bytes=VMEM_LIMIT
        ),
        cost_estimate=pl.CostEstimate(
            flops=2 * rows * width * (width + 3 * units),
            bytes_accessed=2 * width * (width + 3 * units),
            transcendentals=0,
        ),
    )(
        queries,
        lengths,
        residual,
        gain,
        expert_ids.T,
        gate_weights.T,
        owners,
        cache_keys,
        cache_values,
        out_proj,
        gate_proj,
        up_proj,
        down_proj,
    )


def tiles_whole(mesh, operands):
    queries, cache_keys, _, _, out_proj, residual = operands[:6]
    owners, gate_proj = operands[9], operands[10]
    group = queries.shape[1] // (cache_keys.shape[1] * cache_keys.shape[3])
    return (
        mesh.shape["sec"] == 2
        and mesh.shape["dev"] in (4, 8, 16)
        and owners.shape[0] == mesh.shape["dev"]
        and gate_proj.shape[0] == 1
        and group % 16 == 0
        and cache_keys.shape[3] % 128 == 0
        and cache_keys.shape[2] % 128 == 0
        and residual.shape[0] % 16 == 0
        and out_proj.shape[0] % 128 == 0
        and gate_proj.shape[1] % 128 == 0
    )


def solution(mesh):
    in_specs = (
        P("dev", "sec"),
        P("dev", "sec", None, None),
        P("dev", "sec", None, None),
        P("dev"),
        P("dev", "sec"),
        P(None, "dev"),
        P(),
        P(),
        P(),
        P(),
        P("dev", "sec", None),
        P("dev", "sec", None),
        P("dev", "sec", None),
    )
    out_specs = P(None, "dev")

    def chosen(*operands):
        if tiles_whole(mesh, operands):
            return fused(mesh.shape["dev"], *operands)
        return shards(*operands)

    return jax.shard_map(chosen, mesh=mesh, in_specs=in_specs, out_specs=out_specs, check_vma=False)
```

time: 47.2 us -> 39.3 us (0.83); the launches traced: 46.3 us -> 39 us
  local copies, waits for them, and re-layouts: 9.26 us -> 1.32 us
  Pallas kernels: 37 us -> 37.7 us
    unnamed x17 -> x1, local copies, waits for them, and re-layouts: 8.55 us -> 1.32 us
    reshape x1 -> x0, local copies, waits for them, and re-layouts: 0.71 us -> none  [fused(): norm_gain.reshape(1, width)]
    pallas_call x1, Pallas kernels: 37 us -> 37.7 us  [fused(): pl.pallas_call(functools.partial(fused_kernel, n_dev), out_shape=jax.Shap...]
where the time goes in v2:
time: 39.3 us; the launch traced here: 39 us
  Pallas kernels  37.7 us (96%)
  local copies, waits for them, and re-layouts  1.32 us (3%)
    pallas_call x1, Pallas kernels, fused(): pl.pallas_call(functools.partial(fused_kernel, n_dev), out_shape=jax.Shap...  37.7 us
    unnamed x1, local copies, waits for them, and re-layouts  1.32 us

profile of v2, /device:TPU:0, one launch (start us, length us, event | category | flops | bytes accessed | tf_op | source)
XLA Modules:
  0.0 39.0 jit_solution(877362052380386851)
XLA Ops:
  0.0 37.7 %shard_map.127 = bf16[32,256]{1,0:T(8,128)(2,1)} custom-call(bf16[2,4096]{1,0:T(2,128)(2,1)} %queries_hbm.1, s32[2]{0:T(128)} %lengths_hbm.1, bf16[32,256]{1,0:T(8,128)(2,1)} %residual_hbm.1, bf16[4096]{0:T(1024)(128)(2,1)} %gain_hbm.1, s32[8,32]{1,0:T(8,128)} %bitcast.2, f32[8,32]{1,0:T(8,128)} %bitcast.3, s32[16]{0:T(128)} %owners_hbm.1, ...), custom_call_target="tpu_custom_call" | custom-call | flops 1375731712 | bytes 42991616 | tf_op jit(solution)/shard_map/pallas_call | solution.py:440
  37.7 1.3 %copy.15 = bf16[32,256]{1,0:T(8,128)(2,1)} copy(bf16[32,256]{1,0:T(8,128)(2,1)} %shard_map.127) | data formatting | bytes 32768

commit v3 on v2

--- a/solution.py
+++ b/solution.py
@@ -276,28 +276,28 @@
     loads[1].wait()
     loads[3].wait()
     position = lax.broadcasted_iota(jnp.int32, (group, span), 1)
-    scores = []
+    sends = []
     for kv in range(kv_heads):
+        scores = []
         for row in range(rows_here):
             query = query_rows[kv, row * group : (row + 1) * group, :].astype(jnp.bfloat16)
             found = times_transpose(query, keys[row, kv]) * (1.0 / math.sqrt(head_dim))
             scores.append(jnp.where(position < lengths[row], found, -jnp.inf))
-    scores = jnp.concatenate(scores, axis=0)
-    raised = jnp.exp(scores - jnp.max(scores, axis=1, keepdims=True))
-    probs = (raised / jnp.sum(raised, axis=1, keepdims=True)).astype(jnp.bfloat16)
-    loads[2].wait()
-    for kv in range(kv_heads):
+        scores = jnp.concatenate(scores, axis=0)
+        raised = jnp.exp(scores - jnp.max(scores, axis=1, keepdims=True))
+        probs = (raised / jnp.sum(raised, axis=1, keepdims=True)).astype(jnp.bfloat16)
+        if kv == 0:
+            loads[2].wait()
         for row in range(rows_here):
-            block = kv * rows_here + row
             found = jnp.dot(
-                probs[block * group : (block + 1) * group],
+                probs[row * group : (row + 1) * group],
                 values[row, kv],
                 preferred_element_type=jnp.float32,
             )
-            heads_in[dev, block] = found.astype(jnp.bfloat16)
-
-    pl.semaphore_wait(barrier, chips + 1)
-    sends = gather_start(0, heads_in)
+            heads_in[kv, dev, row] = found.astype(jnp.bfloat16)
+        if kv == 0:
+            pl.semaphore_wait(barrier, chips + 1)
+        sends += gather_start(kv, heads_in.at[kv])
 
     for i in (5, 6, 7, 8, 9):
         loads[i].wait()
@@ -313,35 +313,37 @@
         jnp.where(diagonal, jnp.broadcast_to(lying, square), 0.0), axis=1, keepdims=True
     )
 
-    for k in range(1, chips):
-        sends.append(gather_pass(0, heads_in, k))
-    for k in range(chips):
-        landed(0, heads_in, other[k])
+    for kv in range(kv_heads):
+        for k in range(1, chips):
+            sends.append(gather_pass(kv, heads_in.at[kv], k))
     loads[4].wait()
+    part = jnp.zeros((rows, cols), jnp.float32)
     for kv in range(kv_heads):
+        for k in range(chips):
+            landed(kv, heads_in.at[kv], other[k])
         for d in range(n_dev):
             for row in range(rows_here):
                 place = (d * rows_here + row) * group
-                heads_wide[kv, place : place + group, :] = heads_in[
-                    d, kv * rows_here + row
-                ].astype(jnp.float32)
-    features = jnp.concatenate(
-        [
-            heads_wide[kv, pl.ds(g, rows, stride=group), :]
-            for kv in range(kv_heads)
-            for g in range(group)
-        ],
-        axis=1,
-    ).astype(jnp.bfloat16)
-    part = times_transpose(features, out_proj[...])
+                heads_wide[kv, place : place + group, :] = heads_in[kv, d, row].astype(
+                    jnp.float32
+                )
+        features = jnp.concatenate(
+            [heads_wide[kv, pl.ds(g, rows, stride=group), :] for g in range(group)], axis=1
+        ).astype(jnp.bfloat16)
+        part = part + times_transpose(
+            features, out_proj[:, kv * kv_width : (kv + 1) * kv_width]
+        )
+    part = part.astype(jnp.bfloat16)
     part_out[...] = part
     swap = remote(part_out, part_in, pair_sem.at[0, 0], pair_sem.at[0, 1], across)
     swap.start()
     sends.append(swap)
     swap.wait_recv()
-    base = residual[...].astype(jnp.float32) + (part + part_in[...])
+    base = residual[...].astype(jnp.float32) + (
+        part.astype(jnp.float32) + part_in[...].astype(jnp.float32)
+    )
     hidden_in[dev] = base.astype(jnp.bfloat16)
-    sends += gather_start(1, hidden_in)
+    sends += gather_start(kv_heads, hidden_in)
 
     loads[10].wait()
     loads[11].wait()
@@ -358,12 +360,13 @@
         )
 
     squares, raising = take(dev, squares, raising)
-    for k in range(chips):
-        if k:
-            sends.append(gather_pass(1, hidden_in, k))
-            squares, raising = take(same[k], squares, raising)
-        landed(1, hidden_in, other[k])
-        squares, raising = take(other[k], squares, raising)
+    for k in range(1, chips):
+        sends.append(gather_pass(kv_heads, hidden_in, k))
+        landed(kv_heads, hidden_in, other[k - 1])
+        squares, raising = take(same[k], squares, raising)
+        squares, raising = take(other[k - 1], squares, raising)
+    landed(kv_heads, hidden_in, other[chips - 1])
+    squares, raising = take(other[chips - 1], squares, raising)
     square_mean = jnp.sum(squares, axis=1, keepdims=True) / (n_dev * cols)
     raising = raising * lax.rsqrt(square_mean + epsilon)
     gate_act, up_act = raising[:, :units], raising[:, units:]
@@ -375,40 +378,52 @@
         return made * weight
 
     loads[12].wait()
+    halves = (range(chips - 1, chips // 2 - 1, -1), range(chips // 2 - 1, -1, -1))
     crossing = {}
-    for k in reversed(range(chips)):
-        cross_out[k] = lowered(other[k]).astype(jnp.bfloat16)
-        crossing[k] = remote(
-            cross_out.at[k], cross_in.at[k], back_send_sem.at[0, k], back_recv_sem.at[0, k], to_twin
-        )
-        crossing[k].start()
-        sends.append(crossing[k])
+    for half in halves:
+        for k in half:
+            cross_out[k] = lowered(other[k]).astype(jnp.bfloat16)
+        for k in half:
+            crossing[k] = remote(
+                cross_out.at[k], cross_in.at[k], back_send_sem.at[0, k],
+                back_recv_sem.at[0, k], to_twin,
+            )
+            crossing[k].start()
+            sends.append(crossing[k])
     backs = {}
-    for k in reversed(range(chips)):
-        made = lowered(same[k])
-        crossing[k].wait_recv()
-        made = made + cross_in[k].astype(jnp.float32)
-        if k == 0:
-            moe = made
-            continue
-        back_out[k] = made.astype(jnp.bfloat16)
-        backs[k] = remote(
-            back_out.at[k], back_in.at[k], back_send_sem.at[1, k], back_recv_sem.at[1, k],
-            {"dev": same[k]},
-        )
-        backs[k].start()
-        sends.append(backs[k])
+    for half in halves:
+        made = {k: lowered(same[k]) for k in half}
+        for k in half:
+            crossing[k].wait_recv()
+        for k in half:
+            made[k] = made[k] + cross_in[k].astype(jnp.float32)
+            if k:
+                back_out[k] = made[k].astype(jnp.bfloat16)
+        for k in half:
+            if k == 0:
+                continue
+            backs[k] = remote(
+                back_out.at[k], back_in.at[k], back_send_sem.at[1, k],
+                back_recv_sem.at[1, k], {"dev": same[k]},
+            )
+            backs[k].start()
+    moe = made[0]
+    for copy in sends:
+        copy.wait_send()
     for k in range(1, chips):
         backs[k].wait_recv()
         moe = moe + back_in[k].astype(jnp.float32)
+    moe = moe.astype(jnp.bfloat16)
     last_out[...] = moe
     last = remote(last_out, last_in, pair_sem.at[1, 0], pair_sem.at[1, 1], across)
     last.start()
-    sends.append(last)
+    for k in range(1, chips):
+        backs[k].wait_send()
+    last.wait_send()
     last.wait_recv()
-    output[...] = (base + (moe + last_in[...])).astype(jnp.bfloat16)
-    for copy in sends:
-        copy.wait_send()
+    output[...] = (
+        base + (moe.astype(jnp.float32) + last_in[...].astype(jnp.float32))
+    ).astype(jnp.bfloat16)
 
 
 def fused(
@@ -435,7 +450,6 @@
     chips = n_dev // 2
     whole = pl.BlockSpec(memory_space=pltpu.HBM)
     wide, narrow = jnp.float32, jnp.bfloat16
-    blocks = rows_here * kv_heads
     gain = norm_gain
     return pl.pallas_call(
         functools.partial(fused_kernel, n_dev),
@@ -456,21 +470,21 @@
             pltpu.VMEM((2 * units, width), narrow),
             pltpu.VMEM((units, width), narrow),
             pltpu.VMEM((kv_heads, rows_here * group, head_dim), wide),
-            pltpu.VMEM((n_dev, blocks, group, head_dim), narrow),
+            pltpu.VMEM((kv_heads, n_dev, rows_here, group, head_dim), narrow),
             pltpu.VMEM((kv_heads, rows * group, head_dim), wide),
-            pltpu.VMEM((rows, cols), wide),
-            pltpu.VMEM((rows, cols), wide),
+            pltpu.VMEM((rows, cols), narrow),
+            pltpu.VMEM((rows, cols), narrow),
             pltpu.VMEM((n_dev, rows, cols), narrow),
             pltpu.VMEM((chips, rows, cols), narrow),
             pltpu.VMEM((chips, rows, cols), narrow),
             pltpu.VMEM((chips, rows, cols), narrow),
             pltpu.VMEM((chips, rows, cols), narrow),
-            pltpu.VMEM((rows, cols), wide),
-            pltpu.VMEM((rows, cols), wide),
+            pltpu.VMEM((rows, cols), narrow),
+            pltpu.VMEM((rows, cols), narrow),
             pltpu.SemaphoreType.DMA((13,)),
-            pltpu.SemaphoreType.DMA((2, chips)),
-            pltpu.SemaphoreType.DMA((2, n_dev)),
-            pltpu.SemaphoreType.DMA((2, chips)),
+            pltpu.SemaphoreType.DMA((kv_heads + 1, chips)),
+            pltpu.SemaphoreType.DMA((kv_heads + 1, n_dev)),
+            pltpu.SemaphoreType.DMA((kv_heads + 1, chips)),
             pltpu.SemaphoreType.DMA((2, chips)),
             pltpu.SemaphoreType.DMA((2, chips)),
             pltpu.SemaphoreType.DMA((2, 2)),

time: 39.3 us -> 36.4 us (0.926)
  Pallas kernels: 37.7 us -> 34.8 us
    pallas_call x1, Pallas kernels: 37.7 us -> 34.8 us  [fused(): pl.pallas_call(functools.partial(fused_kernel, n_dev), out_shape=jax.Shap...]
where the time goes in v3:
time: 36.4 us; the launch traced here: 36.1 us
  Pallas kernels  34.8 us (96%)
  local copies, waits for them, and re-layouts  1.32 us (4%)
    pallas_call x1, Pallas kernels, fused(): pl.pallas_call(functools.partial(fused_kernel, n_dev), out_shape=jax.Shap...  34.8 us
    unnamed x1, local copies, waits for them, and re-layouts  1.32 us

profile of v3, /device:TPU:0, one launch (start us, length us, event | category | flops | bytes accessed | tf_op | source)
XLA Modules:
  0.0 36.1 jit_solution(5008663242824246613)
XLA Ops:
  0.0 34.8 %shard_map.127 = bf16[32,256]{1,0:T(8,128)(2,1)} custom-call(bf16[2,4096]{1,0:T(2,128)(2,1)} %queries_hbm.1, s32[2]{0:T(128)} %lengths_hbm.1, bf16[32,256]{1,0:T(8,128)(2,1)} %residual_hbm.1, bf16[4096]{0:T(1024)(128)(2,1)} %gain_hbm.1, s32[8,32]{1,0:T(8,128)} %bitcast.2, f32[8,32]{1,0:T(8,128)} %bitcast.3, s32[16]{0:T(128)} %owners_hbm.1, ...), custom_call_target="tpu_custom_call" | custom-call | flops 1375731712 | bytes 42991616 | tf_op jit(solution)/shard_map/pallas_call | solution.py:454
  34.8 1.3 %copy.15 = bf16[32,256]{1,0:T(8,128)(2,1)} copy(bf16[32,256]{1,0:T(8,128)(2,1)} %shard_map.127) | data formatting | bytes 32768

commit v4 on v3

--- a/solution.py
+++ b/solution.py
@@ -158,6 +158,7 @@
     query_rows,
     heads_in,
     heads_wide,
+    part_sum,
     part_out,
     part_in,
     hidden_in,
@@ -171,6 +172,7 @@
     send_sem,
     recv_sem,
     pass_sem,
+    pair_recv_sem,
     back_send_sem,
     back_recv_sem,
     pair_sem,
@@ -186,19 +188,21 @@
     units = down_w.shape[0]
     kv_width = group * head_dim
 
-    def flipped(k):
-        bit, place = 1, 0
-        while bit < chips:
-            place = place + lax.rem(lax.div(chip, bit) + (k // bit) % 2, 2) * bit
+    def flipped(place, k, amount):
+        bit, result = 1, 0
+        while bit < amount:
+            result = result + lax.rem(lax.div(place, bit) + k // bit, 2) * bit
             bit *= 2
-        return place
-
-    chip_of = [flipped(k) for k in range(chips)]
-    twin = 2 * chip + 1 - core
-    to_twin = {"dev": twin}
+        return result
+
+    def chip_of(k):
+        return flipped(chip, k, chips)
+
+    def pair_of(p):
+        return pl.ds(2 * flipped(lax.div(chip, 2), p, chips // 2), 2)
+
+    to_twin = {"dev": 2 * chip + 1 - core}
     across = {"sec": 1 - sec}
-    same = [2 * chip_of[k] + core for k in range(chips)]
-    other = [2 * chip_of[k] + 1 - core for k in range(chips)]
 
     pairs = (
         (queries_hbm, queries),
@@ -223,7 +227,12 @@
         load.start()
 
     barrier = pltpu.get_barrier_semaphore()
-    for place in [across, to_twin] + [{"dev": same[k]} for k in range(1, chips)]:
+    for place in (across, to_twin):
+        pl.semaphore_signal(barrier, inc=1, device_id=place, device_id_type=MESH)
+
+    @pl.loop(1, chips)
+    def _(k):
+        place = {"dev": 2 * chip_of(k) + core}
         pl.semaphore_signal(barrier, inc=1, device_id=place, device_id_type=MESH)
 
     def remote(source, target, sent, received, place):
@@ -236,33 +245,48 @@
             device_id_type=MESH,
         )
 
-    def landed(phase, buffer, index):
+    def sending(phase, buffer, k):
+        own = buffer.at[core, chip]
+        return remote(
+            own, own, send_sem.at[phase, k], recv_sem.at[phase, chip],
+            {"dev": 2 * chip_of(k) + core},
+        )
+
+    def gather_start(phase, buffer):
+        @pl.loop(1, chips)
+        def _(step):
+            sending(phase, buffer, chips - step).start()
+
+    def passing(phase, buffer, p):
+        pair = buffer.at[core, pair_of(p)]
+        return remote(pair, pair, pass_sem.at[phase, p], pair_recv_sem.at[phase, p], to_twin)
+
+    def arriving(phase, buffer, k):
+        block = buffer.at[core, chip_of(k)]
         remote(
-            buffer.at[index], buffer.at[index], send_sem.at[phase, 0],
-            recv_sem.at[phase, index], to_twin,
+            block, block, send_sem.at[phase, 0], recv_sem.at[phase, chip_of(k)], to_twin
         ).wait_recv()
 
-    def gather_start(phase, buffer):
-        copies = []
-        for k in reversed(range(chips)):
-            place = {"dev": same[k]} if k else to_twin
-            copies.append(
-                remote(
-                    buffer.at[dev], buffer.at[dev], send_sem.at[phase, k],
-                    recv_sem.at[phase, dev], place,
-                )
-            )
-            copies[-1].start()
-        return copies
-
-    def gather_pass(phase, buffer, k):
-        landed(phase, buffer, same[k])
-        copy = remote(
-            buffer.at[same[k]], buffer.at[same[k]], pass_sem.at[phase, k],
-            recv_sem.at[phase, same[k]], to_twin,
-        )
-        copy.start()
-        return copy
+    def gather_pass(phase, buffer, p):
+        for k in (2 * p, 2 * p + 1):
+            if not isinstance(k, int) or k:
+                arriving(phase, buffer, k)
+        passing(phase, buffer, p).start()
+
+    def landed(phase, buffer, p):
+        pair = buffer.at[1 - core, pair_of(p)]
+        remote(
+            pair, pair, pass_sem.at[phase, p], pair_recv_sem.at[phase, p], to_twin
+        ).wait_recv()
+
+    def gather_sent(phase, buffer):
+        @pl.loop(1, chips)
+        def _(k):
+            sending(phase, buffer, k).wait_send()
+
+        @pl.loop(0, chips // 2)
+        def _(p):
+            passing(phase, buffer, p).wait_send()
 
     loads[0].wait()
     wide_queries = queries[...].astype(jnp.float32)
@@ -275,9 +299,12 @@
                 ]
     loads[1].wait()
     loads[3].wait()
+    loads[2].wait()
+    pl.semaphore_wait(barrier, chips + 1)
     position = lax.broadcasted_iota(jnp.int32, (group, span), 1)
-    sends = []
-    for kv in range(kv_heads):
+
+    @pl.loop(0, kv_heads)
+    def _(kv):
         scores = []
         for row in range(rows_here):
             query = query_rows[kv, row * group : (row + 1) * group, :].astype(jnp.bfloat16)
@@ -286,18 +313,14 @@
         scores = jnp.concatenate(scores, axis=0)
         raised = jnp.exp(scores - jnp.max(scores, axis=1, keepdims=True))
         probs = (raised / jnp.sum(raised, axis=1, keepdims=True)).astype(jnp.bfloat16)
-        if kv == 0:
-            loads[2].wait()
         for row in range(rows_here):
             found = jnp.dot(
                 probs[row * group : (row + 1) * group],
                 values[row, kv],
                 preferred_element_type=jnp.float32,
             )
-            heads_in[kv, dev, row] = found.astype(jnp.bfloat16)
-        if kv == 0:
-            pl.semaphore_wait(barrier, chips + 1)
-        sends += gather_start(kv, heads_in.at[kv])
+            heads_in[kv, core, chip, row] = found.astype(jnp.bfloat16)
+        gather_start(kv, heads_in.at[kv])
 
     for i in (5, 6, 7, 8, 9):
         loads[i].wait()
@@ -313,117 +336,148 @@
         jnp.where(diagonal, jnp.broadcast_to(lying, square), 0.0), axis=1, keepdims=True
     )
 
-    for kv in range(kv_heads):
-        for k in range(1, chips):
-            sends.append(gather_pass(kv, heads_in.at[kv], k))
+    @pl.loop(0, kv_heads)
+    def _(kv):
+        gather_pass(kv, heads_in.at[kv], 0)
+
+        @pl.loop(1, chips // 2)
+        def _(p):
+            gather_pass(kv, heads_in.at[kv], p)
+
     loads[4].wait()
-    part = jnp.zeros((rows, cols), jnp.float32)
-    for kv in range(kv_heads):
-        for k in range(chips):
-            landed(kv, heads_in.at[kv], other[k])
+    part_sum[...] = jnp.zeros((rows, cols), jnp.float32)
+
+    @pl.loop(0, kv_heads)
+    def _(kv):
+        @pl.loop(0, chips // 2)
+        def _(p):
+            landed(kv, heads_in.at[kv], p)
+
         for d in range(n_dev):
             for row in range(rows_here):
                 place = (d * rows_here + row) * group
-                heads_wide[kv, place : place + group, :] = heads_in[kv, d, row].astype(
+                heads_wide[place : place + group, :] = heads_in[kv, d % 2, d // 2, row].astype(
                     jnp.float32
                 )
         features = jnp.concatenate(
-            [heads_wide[kv, pl.ds(g, rows, stride=group), :] for g in range(group)], axis=1
+            [heads_wide[pl.ds(g, rows, stride=group), :] for g in range(group)], axis=1
         ).astype(jnp.bfloat16)
-        part = part + times_transpose(
-            features, out_proj[:, kv * kv_width : (kv + 1) * kv_width]
-        )
-    part = part.astype(jnp.bfloat16)
+        start = pl.multiple_of(kv * kv_width, kv_width)
+        part_sum[...] += times_transpose(features, out_proj[:, pl.ds(start, kv_width)])
+
+    part = part_sum[...].astype(jnp.bfloat16)
     part_out[...] = part
     swap = remote(part_out, part_in, pair_sem.at[0, 0], pair_sem.at[0, 1], across)
     swap.start()
-    sends.append(swap)
     swap.wait_recv()
     base = residual[...].astype(jnp.float32) + (
         part.astype(jnp.float32) + part_in[...].astype(jnp.float32)
     )
-    hidden_in[dev] = base.astype(jnp.bfloat16)
-    sends += gather_start(kv_heads, hidden_in)
+    hidden_in[core, chip] = base.astype(jnp.bfloat16)
+    gather_start(kv_heads, hidden_in)
 
     loads[10].wait()
     loads[11].wait()
     squares = jnp.zeros((rows, cols), jnp.float32)
     raising = jnp.zeros((rows, 2 * units), jnp.float32)
 
-    def take(index, squares, raising):
-        start = pl.multiple_of(index * cols, cols)
-        block = hidden_in[index].astype(jnp.float32)
-        scaled = (block * gain[pl.ds(start, cols)].astype(jnp.float32).reshape(1, cols)).astype(jnp.bfloat16)
-        return (
-            squares + block * block,
-            raising + times_transpose(scaled, rising[:, pl.ds(start, cols)]),
-        )
-
-    squares, raising = take(dev, squares, raising)
-    for k in range(1, chips):
-        sends.append(gather_pass(kv_heads, hidden_in, k))
-        landed(kv_heads, hidden_in, other[k - 1])
-        squares, raising = take(same[k], squares, raising)
-        squares, raising = take(other[k - 1], squares, raising)
-    landed(kv_heads, hidden_in, other[chips - 1])
-    squares, raising = take(other[chips - 1], squares, raising)
+    def take(side, p, squares, raising):
+        first = pair_of(p).start
+        for half in range(2):
+            start = pl.multiple_of((2 * (first + half) + side) * cols, cols)
+            block = hidden_in[side, first + half].astype(jnp.float32)
+            scale = gain[pl.ds(start, cols)].astype(jnp.float32).reshape(1, cols)
+            scaled = (block * scale).astype(jnp.bfloat16)
+            squares = squares + block * block
+            raising = raising + times_transpose(scaled, rising[:, pl.ds(start, cols)])
+        return squares, raising
+
+    gather_pass(kv_heads, hidden_in, 0)
+    squares, raising = take(core, 0, squares, raising)
+
+    def stage(p, carried):
+        gather_pass(kv_heads, hidden_in, p)
+        landed(kv_heads, hidden_in, p - 1)
+        return take(1 - core, p - 1, *take(core, p, *carried))
+
+    squares, raising = lax.fori_loop(1, chips // 2, stage, (squares, raising))
+    landed(kv_heads, hidden_in, chips // 2 - 1)
+    squares, raising = take(1 - core, chips // 2 - 1, squares, raising)
     square_mean = jnp.sum(squares, axis=1, keepdims=True) / (n_dev * cols)
     raising = raising * lax.rsqrt(square_mean + epsilon)
     gate_act, up_act = raising[:, :units], raising[:, units:]
     act = (gate_act * (1.0 / (1.0 + jnp.exp(-gate_act))) * up_act).astype(jnp.bfloat16)
 
-    def lowered(index):
-        start = pl.multiple_of(index * cols, cols)
+    def lowered(side, k):
+        start = pl.multiple_of((2 * chip_of(k) + side) * cols, cols)
         made = jnp.dot(act, down_w[:, pl.ds(start, cols)], preferred_element_type=jnp.float32)
         return made * weight
 
     loads[12].wait()
-    halves = (range(chips - 1, chips // 2 - 1, -1), range(chips // 2 - 1, -1, -1))
-    crossing = {}
-    for half in halves:
-        for k in half:
-            cross_out[k] = lowered(other[k]).astype(jnp.bfloat16)
-        for k in half:
-            crossing[k] = remote(
-                cross_out.at[k], cross_in.at[k], back_send_sem.at[0, k],
-                back_recv_sem.at[0, k], to_twin,
-            )
-            crossing[k].start()
-            sends.append(crossing[k])
-    backs = {}
-    for half in halves:
-        made = {k: lowered(same[k]) for k in half}
-        for k in half:
-            crossing[k].wait_recv()
-        for k in half:
-            made[k] = made[k] + cross_in[k].astype(jnp.float32)
-            if k:
-                back_out[k] = made[k].astype(jnp.bfloat16)
-        for k in half:
-            if k == 0:
-                continue
-            backs[k] = remote(
-                back_out.at[k], back_in.at[k], back_send_sem.at[1, k],
-                back_recv_sem.at[1, k], {"dev": same[k]},
-            )
-            backs[k].start()
-    moe = made[0]
-    for copy in sends:
-        copy.wait_send()
-    for k in range(1, chips):
-        backs[k].wait_recv()
-        moe = moe + back_in[k].astype(jnp.float32)
+    batch = chips // 2
+
+    def crossing(h):
+        part = pl.ds(h * batch, batch)
+        return remote(
+            cross_out.at[part], cross_in.at[part], back_send_sem.at[0, h],
+            back_recv_sem.at[0, h], to_twin,
+        )
+
+    def backing(k):
+        return remote(
+            back_out.at[k], back_in.at[k], back_send_sem.at[1, k], back_recv_sem.at[1, k],
+            {"dev": 2 * chip_of(k) + core},
+        )
+
+    @pl.loop(0, 2)
+    def _(step):
+        h = 1 - step
+        for i in range(batch):
+            k = h * batch + i
+            cross_out[k] = lowered(1 - core, k).astype(jnp.bfloat16)
+        crossing(h).start()
+
+    @pl.loop(0, 2)
+    def _(step):
+        h = 1 - step
+        made = [lowered(core, h * batch + i) for i in range(batch)]
+        crossing(h).wait_recv()
+        for i in range(batch):
+            k = h * batch + i
+            back_out[k] = (made[i] + cross_in[k].astype(jnp.float32)).astype(jnp.bfloat16)
+
+        @pl.loop(h * batch + step, (h + 1) * batch)
+        def _(k):
+            backing(k).start()
+
+    @pl.loop(0, kv_heads)
+    def _(kv):
+        gather_sent(kv, heads_in.at[kv])
+
+    gather_sent(kv_heads, hidden_in)
+    swap.wait_send()
+
+    @pl.loop(0, 2)
+    def _(h):
+        crossing(h).wait_send()
+
+    def collect(k, moe):
+        backing(k).wait_recv()
+        return moe + back_in[k].astype(jnp.float32)
+
+    moe = lax.fori_loop(1, chips, collect, back_out[0].astype(jnp.float32))
     moe = moe.astype(jnp.bfloat16)
     last_out[...] = moe
     last = remote(last_out, last_in, pair_sem.at[1, 0], pair_sem.at[1, 1], across)
     last.start()
-    for k in range(1, chips):
-        backs[k].wait_send()
+
+    @pl.loop(1, chips)
+    def _(k):
+        backing(k).wait_send()
+
     last.wait_send()
     last.wait_recv()
-    output[...] = (
-        base + (moe.astype(jnp.float32) + last_in[...].astype(jnp.float32))
-    ).astype(jnp.bfloat16)
+    output[...] = base + (moe.astype(jnp.float32) + last_in[...].astype(jnp.float32))
 
 
 def fused(
@@ -453,7 +507,7 @@
     gain = norm_gain
     return pl.pallas_call(
         functools.partial(fused_kernel, n_dev),
-        out_shape=jax.ShapeDtypeStruct((rows, cols), narrow),
+        out_shape=jax.ShapeDtypeStruct((rows, cols), wide),
         in_specs=[whole] * 13,
         out_specs=pl.BlockSpec(memory_space=pltpu.VMEM),
         scratch_shapes=[
@@ -470,11 +524,12 @@
             pltpu.VMEM((2 * units, width), narrow),
             pltpu.VMEM((units, width), narrow),
             pltpu.VMEM((kv_heads, rows_here * group, head_dim), wide),
-            pltpu.VMEM((kv_heads, n_dev, rows_here, group, head_dim), narrow),
-            pltpu.VMEM((kv_heads, rows * group, head_dim), wide),
+            pltpu.VMEM((kv_heads, 2, chips, rows_here, group, head_dim), narrow),
+            pltpu.VMEM((rows * group, head_dim), wide),
+            pltpu.VMEM((rows, cols), wide),
             pltpu.VMEM((rows, cols), narrow),
             pltpu.VMEM((rows, cols), narrow),
-            pltpu.VMEM((n_dev, rows, cols), narrow),
+            pltpu.VMEM((2, chips, rows, cols), narrow),
             pltpu.VMEM((chips, rows, cols), narrow),
             pltpu.VMEM((chips, rows, cols), narrow),
             pltpu.VMEM((chips, rows, cols), narrow),
@@ -483,8 +538,9 @@
             pltpu.VMEM((rows, cols), narrow),
             pltpu.SemaphoreType.DMA((13,)),
             pltpu.SemaphoreType.DMA((kv_heads + 1, chips)),
-            pltpu.SemaphoreType.DMA((kv_heads + 1, n_dev)),
             pltpu.SemaphoreType.DMA((kv_heads + 1, chips)),
+            pltpu.SemaphoreType.DMA((kv_heads + 1, chips // 2)),
+            pltpu.SemaphoreType.DMA((kv_heads + 1, chips // 2)),
             pltpu.SemaphoreType.DMA((2, chips)),
             pltpu.SemaphoreType.DMA((2, chips)),
             pltpu.SemaphoreType.DMA((2, 2)),
@@ -511,7 +567,7 @@
         gate_proj,
         up_proj,
         down_proj,
-    )
+    ).astype(narrow)
 
 
 def tiles_whole(mesh, operands):

time: 36.4 us -> 34.5 us (0.948)
  Pallas kernels: 34.8 us -> 32.8 us
  other arithmetic: 0 us -> 1.37 us
  local copies, waits for them, and re-layouts: 1.32 us -> 0 us
    pallas_call x1, Pallas kernels: 34.8 us -> 32.8 us  [fused(): pl.pallas_call(functools.partial(fused_kernel, n_dev), out_shape=jax.Shap...]
    convert_element_type x0 -> x1, other arithmetic: none -> 1.37 us  [fused(): return pl.pallas_call(functools.partial(fused_kernel, n_dev), out_shape=j...]
    unnamed x1 -> x0, local copies, waits for them, and re-layouts: 1.32 us -> none
where the time goes in v4:
time: 34.5 us; the launch traced here: 34.2 us
  Pallas kernels  32.8 us (95%)
  other arithmetic  1.37 us (4%)
    pallas_call x1, Pallas kernels, fused(): pl.pallas_call(functools.partial(fused_kernel, n_dev), out_shape=jax.Shap...  32.8 us
    convert_element_type x1, other arithmetic, fused(): return pl.pallas_call(functools.partial(fused_kernel, n_dev), out_shape=j...  1.37 us

profile of v4, /device:TPU:0, one launch (start us, length us, event | category | flops | bytes accessed | tf_op | source)
XLA Modules:
  0.0 34.2 jit_solution(2107818825563256095)
XLA Ops:
  0.0 32.8 %shard_map.127 = f32[32,256]{1,0:T(8,128)} custom-call(bf16[2,4096]{1,0:T(2,128)(2,1)} %queries_hbm.1, s32[2]{0:T(128)} %lengths_hbm.1, bf16[32,256]{1,0:T(8,128)(2,1)} %residual_hbm.1, bf16[4096]{0:T(1024)(128)(2,1)} %gain_hbm.1, s32[8,32]{1,0:T(8,128)} %bitcast.2, f32[8,32]{1,0:T(8,128)} %bitcast.3, s32[16]{0:T(128)} %owners_hbm.1, ...), custom_call_target="tpu_custom_call" | custom-call | flops 1375731712 | bytes 42991616 | tf_op jit(solution)/shard_map/pallas_call | solution.py:508
  32.9 1.4 %convert_element_type.3 = bf16[32,256]{1,0:T(8,128)(2,1)} convert(f32[32,256]{1,0:T(8,128)} %shard_map.127) | non-fusion elementwise | flops 8192 | bytes 49152 | tf_op jit(solution)/shard_map/convert_element_type | solution.py:570

commit v5 on v4

--- a/solution.py
+++ b/solution.py
@@ -124,7 +124,7 @@
     )
     summed = lax.psum(moe, "sec")
     return (residual_wide + attention_out + summed).astype(jnp.bfloat16)
-VMEM_LIMIT = 64 * 1024 * 1024 - 64 * 1024
+VMEM_LIMIT = 32 * 1024 * 1024
 
 
 def fused_kernel(
@@ -223,8 +223,10 @@
         pltpu.make_async_copy(source, target, load_sem.at[i])
         for i, (source, target) in enumerate(pairs)
     ]
-    for load in loads:
-        load.start()
+    large = (4, 10, 11, 12)
+    for i, load in enumerate(loads):
+        if i not in large:
+            load.start()
 
     barrier = pltpu.get_barrier_semaphore()
     for place in (across, to_twin):
@@ -300,6 +302,8 @@
     loads[1].wait()
     loads[3].wait()
     loads[2].wait()
+    for i in large:
+        loads[i].start()
     pl.semaphore_wait(barrier, chips + 1)
     position = lax.broadcasted_iota(jnp.int32, (group, span), 1)
 
@@ -477,7 +481,9 @@
 
     last.wait_send()
     last.wait_recv()
-    output[...] = base + (moe.astype(jnp.float32) + last_in[...].astype(jnp.float32))
+    output[...] = (
+        base + (moe.astype(jnp.float32) + last_in[...].astype(jnp.float32))
+    ).astype(jnp.bfloat16)
 
 
 def fused(
@@ -505,9 +511,24 @@
     whole = pl.BlockSpec(memory_space=pltpu.HBM)
     wide, narrow = jnp.float32, jnp.bfloat16
     gain = norm_gain
+    operands = (
+        queries,
+        lengths,
+        residual,
+        gain,
+        expert_ids.T,
+        gate_weights.T,
+        owners,
+        cache_keys,
+        cache_values,
+        out_proj,
+        gate_proj,
+        up_proj,
+        down_proj,
+    )
     return pl.pallas_call(
         functools.partial(fused_kernel, n_dev),
-        out_shape=jax.ShapeDtypeStruct((rows, cols), wide),
+        out_shape=pltpu.VMEM((rows, cols), narrow),
         in_specs=[whole] * 13,
         out_specs=pl.BlockSpec(memory_space=pltpu.VMEM),
         scratch_shapes=[
@@ -553,21 +574,7 @@
             bytes_accessed=2 * width * (width + 3 * units),
             transcendentals=0,
         ),
-    )(
-        queries,
-        lengths,
-        residual,
-        gain,
-        expert_ids.T,
-        gate_weights.T,
-        owners,
-        cache_keys,
-        cache_values,
-        out_proj,
-        gate_proj,
-        up_proj,
-        down_proj,
-    ).astype(narrow)
+    )(*(pltpu.with_memory_space_constraint(operand, pltpu.HBM) for operand in operands))
 
 
 def tiles_whole(mesh, operands):

time: 34.5 us -> 33.1 us (0.959)
  other arithmetic: 1.37 us -> 0 us
  local copies, waits for them, and re-layouts: 0 us -> 0.61 us
  Pallas kernels: 32.8 us -> 32.2 us
    convert_element_type x1 -> x0, other arithmetic: 1.37 us -> none  [fused(): return pl.pallas_call(functools.partial(fused_kernel, n_dev), out_shape=j...]
    pallas_call x1, Pallas kernels: 32.8 us -> 32.2 us  [fused(): pl.pallas_call(functools.partial(fused_kernel, n_dev), out_shape=pltpu.VM...]
    unnamed x0 -> x1, local copies, waits for them, and re-layouts: none -> 0.61 us
where the time goes in v5:
time: 33.1 us; the launch traced here: 32.9 us
  Pallas kernels  32.2 us (97%)
  local copies, waits for them, and re-layouts  0.61 us (2%)
    pallas_call x1, Pallas kernels, fused(): pl.pallas_call(functools.partial(fused_kernel, n_dev), out_shape=pltpu.VM...  32.2 us

profile of v5, /device:TPU:0, one launch (start us, length us, event | category | flops | bytes accessed | tf_op | source)
XLA Modules:
  0.0 32.9 jit_solution(14400675821955574730)
XLA Ops:
  0.0 32.2 %shard_map.127 = bf16[32,256]{1,0:T(8,128)(2,1)S(1)} custom-call(bf16[2,4096]{1,0:T(2,128)(2,1)} %queries_hbm.1, s32[2]{0:T(128)} %lengths_hbm.1, bf16[32,256]{1,0:T(8,128)(2,1)} %residual_hbm.1, bf16[4096]{0:T(1024)(128)(2,1)} %gain_hbm.1, s32[8,32]{1,0:T(8,128)} %bitcast.2, f32[8,32]{1,0:T(8,128)} %bitcast.3, s32[16]{0:T(128)} %owners_hbm.1, ...), custom_call_target="tpu_custom_call" | custom-call | flops 1375731712 | bytes 42991616 | tf_op jit(solution)/shard_map/pallas_call | solution.py:529
  32.2 0.6 %copy.15 = bf16[32,256]{1,0:T(8,128)(2,1)} copy(bf16[32,256]{1,0:T(8,128)(2,1)S(1)} %shard_map.127) | data formatting | bytes 32768

commit v6 on v5

--- a/solution.py
+++ b/solution.py
@@ -255,9 +255,19 @@
         )
 
     def gather_start(phase, buffer):
-        @pl.loop(1, chips)
+        @pl.loop(1, chips // 2)
         def _(step):
-            sending(phase, buffer, chips - step).start()
+            sending(phase, buffer, chips - 2 * step).start()
+
+        sending(phase, buffer, 1).start()
+
+    def relaying(phase, buffer, p):
+        place = chip_of(2 * p)
+        block = buffer.at[core, place]
+        return remote(
+            block, block, send_sem.at[phase, 2 * p + 1], recv_sem.at[phase, place],
+            {"dev": 2 * chip_of(1) + core},
+        )
 
     def passing(phase, buffer, p):
         pair = buffer.at[core, pair_of(p)]
@@ -269,10 +279,12 @@
             block, block, send_sem.at[phase, 0], recv_sem.at[phase, chip_of(k)], to_twin
         ).wait_recv()
 
+    def gather_relay(phase, buffer, p):
+        arriving(phase, buffer, 2 * p)
+        relaying(phase, buffer, p).start()
+
     def gather_pass(phase, buffer, p):
-        for k in (2 * p, 2 * p + 1):
-            if not isinstance(k, int) or k:
-                arriving(phase, buffer, k)
+        arriving(phase, buffer, 2 * p + 1)
         passing(phase, buffer, p).start()
 
     def landed(phase, buffer, p):
@@ -282,9 +294,12 @@
         ).wait_recv()
 
     def gather_sent(phase, buffer):
-        @pl.loop(1, chips)
-        def _(k):
-            sending(phase, buffer, k).wait_send()
+        sending(phase, buffer, 1).wait_send()
+
+        @pl.loop(1, chips // 2)
+        def _(p):
+            sending(phase, buffer, 2 * p).wait_send()
+            relaying(phase, buffer, p).wait_send()
 
         @pl.loop(0, chips // 2)
         def _(p):
@@ -342,6 +357,12 @@
 
     @pl.loop(0, kv_heads)
     def _(kv):
+        @pl.loop(1, chips // 2)
+        def _(p):
+            gather_relay(kv, heads_in.at[kv], p)
+
+    @pl.loop(0, kv_heads)
+    def _(kv):
         gather_pass(kv, heads_in.at[kv], 0)
 
         @pl.loop(1, chips // 2)
@@ -396,10 +417,15 @@
             raising = raising + times_transpose(scaled, rising[:, pl.ds(start, cols)])
         return squares, raising
 
+    gather_relay(kv_heads, hidden_in, 1)
     gather_pass(kv_heads, hidden_in, 0)
     squares, raising = take(core, 0, squares, raising)
 
     def stage(p, carried):
+        @pl.when(p < chips // 2 - 1)
+        def _():
+            gather_relay(kv_heads, hidden_in, p + 1)
+
         gather_pass(kv_heads, hidden_in, p)
         landed(kv_heads, hidden_in, p - 1)
         return take(1 - core, p - 1, *take(core, p, *carried))

time: 33.1 us -> 38.4 us (1.16)
  Pallas kernels: 32.2 us -> 37.6 us
    pallas_call x1, Pallas kernels: 32.2 us -> 37.6 us  [fused(): pl.pallas_call(functools.partial(fused_kernel, n_dev), out_shape=pltpu.VM...]
where the time goes in v6:
time: 38.4 us; the launch traced here: 38.2 us
  Pallas kernels  37.6 us (98%)
  local copies, waits for them, and re-layouts  0.61 us (2%)
    pallas_call x1, Pallas kernels, fused(): pl.pallas_call(functools.partial(fused_kernel, n_dev), out_shape=pltpu.VM...  37.6 us

profile of v6, /device:TPU:0, one launch (start us, length us, event | category | flops | bytes accessed | tf_op | source)
XLA Modules:
  0.0 38.2 jit_solution(13338778259475933025)
XLA Ops:
  0.0 37.6 %shard_map.127 = bf16[32,256]{1,0:T(8,128)(2,1)S(1)} custom-call(bf16[2,4096]{1,0:T(2,128)(2,1)} %queries_hbm.1, s32[2]{0:T(128)} %lengths_hbm.1, bf16[32,256]{1,0:T(8,128)(2,1)} %residual_hbm.1, bf16[4096]{0:T(1024)(128)(2,1)} %gain_hbm.1, s32[8,32]{1,0:T(8,128)} %bitcast.2, f32[8,32]{1,0:T(8,128)} %bitcast.3, s32[16]{0:T(128)} %owners_hbm.1, ...), custom_call_target="tpu_custom_call" | custom-call | flops 1375731712 | bytes 42991616 | tf_op jit(solution)/shard_map/pallas_call | solution.py:555
  37.6 0.6 %copy.15 = bf16[32,256]{1,0:T(8,128)(2,1)} copy(bf16[32,256]{1,0:T(8,128)(2,1)S(1)} %shard_map.127) | data formatting | bytes 32768

commit v7 on v5

--- a/solution.py
+++ b/solution.py
@@ -171,8 +171,6 @@
     load_sem,
     send_sem,
     recv_sem,
-    pass_sem,
-    pair_recv_sem,
     back_send_sem,
     back_recv_sem,
     pair_sem,
@@ -198,8 +196,9 @@
     def chip_of(k):
         return flipped(chip, k, chips)
 
-    def pair_of(p):
-        return pl.ds(2 * flipped(lax.div(chip, 2), p, chips // 2), 2)
+    def device_of(k):
+        place = flipped(dev, k, n_dev)
+        return lax.div(place, 2), lax.rem(place, 2)
 
     to_twin = {"dev": 2 * chip + 1 - core}
     across = {"sec": 1 - sec}
@@ -229,12 +228,11 @@
             load.start()
 
     barrier = pltpu.get_barrier_semaphore()
-    for place in (across, to_twin):
-        pl.semaphore_signal(barrier, inc=1, device_id=place, device_id_type=MESH)
-
-    @pl.loop(1, chips)
+    pl.semaphore_signal(barrier, inc=1, device_id=across, device_id_type=MESH)
+
+    @pl.loop(1, n_dev)
     def _(k):
-        place = {"dev": 2 * chip_of(k) + core}
+        place = {"dev": flipped(dev, k, n_dev)}
         pl.semaphore_signal(barrier, inc=1, device_id=place, device_id_type=MESH)
 
     def remote(source, target, sent, received, place):
@@ -250,45 +248,26 @@
     def sending(phase, buffer, k):
         own = buffer.at[core, chip]
         return remote(
-            own, own, send_sem.at[phase, k], recv_sem.at[phase, chip],
-            {"dev": 2 * chip_of(k) + core},
+            own, own, send_sem.at[phase, k], recv_sem.at[phase, k],
+            {"dev": flipped(dev, k, n_dev)},
         )
 
     def gather_start(phase, buffer):
-        @pl.loop(1, chips)
+        @pl.loop(1, n_dev)
         def _(step):
-            sending(phase, buffer, chips - step).start()
-
-    def passing(phase, buffer, p):
-        pair = buffer.at[core, pair_of(p)]
-        return remote(pair, pair, pass_sem.at[phase, p], pair_recv_sem.at[phase, p], to_twin)
-
-    def arriving(phase, buffer, k):
-        block = buffer.at[core, chip_of(k)]
+            sending(phase, buffer, n_dev - step).start()
+
+    def landed(phase, buffer, k):
+        place, side = device_of(k)
+        block = buffer.at[side, place]
         remote(
-            block, block, send_sem.at[phase, 0], recv_sem.at[phase, chip_of(k)], to_twin
+            block, block, send_sem.at[phase, k], recv_sem.at[phase, k], to_twin
         ).wait_recv()
 
-    def gather_pass(phase, buffer, p):
-        for k in (2 * p, 2 * p + 1):
-            if not isinstance(k, int) or k:
-                arriving(phase, buffer, k)
-        passing(phase, buffer, p).start()
-
-    def landed(phase, buffer, p):
-        pair = buffer.at[1 - core, pair_of(p)]
-        remote(
-            pair, pair, pass_sem.at[phase, p], pair_recv_sem.at[phase, p], to_twin
-        ).wait_recv()
-
     def gather_sent(phase, buffer):
-        @pl.loop(1, chips)
+        @pl.loop(1, n_dev)
         def _(k):
             sending(phase, buffer, k).wait_send()
-
-        @pl.loop(0, chips // 2)
-        def _(p):
-            passing(phase, buffer, p).wait_send()
 
     loads[0].wait()
     wide_queries = queries[...].astype(jnp.float32)
@@ -304,7 +283,7 @@
     loads[2].wait()
     for i in large:
         loads[i].start()
-    pl.semaphore_wait(barrier, chips + 1)
+    pl.semaphore_wait(barrier, n_dev)
     position = lax.broadcasted_iota(jnp.int32, (group, span), 1)
 
     @pl.loop(0, kv_heads)
@@ -340,22 +319,14 @@
         jnp.where(diagonal, jnp.broadcast_to(lying, square), 0.0), axis=1, keepdims=True
     )
 
+    loads[4].wait()
+    part_sum[...] = jnp.zeros((rows, cols), jnp.float32)
+
     @pl.loop(0, kv_heads)
     def _(kv):
-        gather_pass(kv, heads_in.at[kv], 0)
-
-        @pl.loop(1, chips // 2)
-        def _(p):
-            gather_pass(kv, heads_in.at[kv], p)
-
-    loads[4].wait()
-    part_sum[...] = jnp.zeros((rows, cols), jnp.float32)
-
-    @pl.loop(0, kv_heads)
-    def _(kv):
-        @pl.loop(0, chips // 2)
-        def _(p):
-            landed(kv, heads_in.at[kv], p)
+        @pl.loop(1, n_dev)
+        def _(k):
+            landed(kv, heads_in.at[kv], k)
 
         for d in range(n_dev):
             for row in range(rows_here):
@@ -385,28 +356,33 @@
     squares = jnp.zeros((rows, cols), jnp.float32)
     raising = jnp.zeros((rows, 2 * units), jnp.float32)
 
-    def take(side, p, squares, raising):
-        first = pair_of(p).start
-        for half in range(2):
-            start = pl.multiple_of((2 * (first + half) + side) * cols, cols)
-            block = hidden_in[side, first + half].astype(jnp.float32)
-            scale = gain[pl.ds(start, cols)].astype(jnp.float32).reshape(1, cols)
-            scaled = (block * scale).astype(jnp.bfloat16)
-            squares = squares + block * block
-            raising = raising + times_transpose(scaled, rising[:, pl.ds(start, cols)])
-        return squares, raising
-
-    gather_pass(kv_heads, hidden_in, 0)
-    squares, raising = take(core, 0, squares, raising)
-
-    def stage(p, carried):
-        gather_pass(kv_heads, hidden_in, p)
-        landed(kv_heads, hidden_in, p - 1)
-        return take(1 - core, p - 1, *take(core, p, *carried))
-
-    squares, raising = lax.fori_loop(1, chips // 2, stage, (squares, raising))
-    landed(kv_heads, hidden_in, chips // 2 - 1)
-    squares, raising = take(1 - core, chips // 2 - 1, squares, raising)
+    batch = n_dev // 4
+
+    def take(k, squares, raising):
+        place, side = device_of(k)
+        start = pl.multiple_of((2 * place + side) * cols, cols)
+        block = hidden_in[side, place].astype(jnp.float32)
+        scale = gain[pl.ds(start, cols)].astype(jnp.float32).reshape(1, cols)
+        scaled = (block * scale).astype(jnp.bfloat16)
+        return (
+            squares + block * block,
+            raising + times_transpose(scaled, rising[:, pl.ds(start, cols)]),
+        )
+
+    def stage(j, carried):
+        @pl.when(j > 0)
+        def _():
+            landed(kv_heads, hidden_in, j * batch)
+
+        @pl.loop(1, batch)
+        def _(i):
+            landed(kv_heads, hidden_in, j * batch + i)
+
+        for i in range(batch):
+            carried = take(j * batch + i, *carried)
+        return carried
+
+    squares, raising = lax.fori_loop(0, 4, stage, (squares, raising))
     square_mean = jnp.sum(squares, axis=1, keepdims=True) / (n_dev * cols)
     raising = raising * lax.rsqrt(square_mean + epsilon)
     gate_act, up_act = raising[:, :units], raising[:, units:]
@@ -558,10 +534,8 @@
             pltpu.VMEM((rows, cols), narrow),
             pltpu.VMEM((rows, cols), narrow),
             pltpu.SemaphoreType.DMA((13,)),
-            pltpu.SemaphoreType.DMA((kv_heads + 1, chips)),
-            pltpu.SemaphoreType.DMA((kv_heads + 1, chips)),
-            pltpu.SemaphoreType.DMA((kv_heads + 1, chips // 2)),
-            pltpu.SemaphoreType.DMA((kv_heads + 1, chips // 2)),
+            pltpu.SemaphoreType.DMA((kv_heads + 1, n_dev)),
+            pltpu.SemaphoreType.DMA((kv_heads + 1, n_dev)),
             pltpu.SemaphoreType.DMA((2, chips)),
             pltpu.SemaphoreType.DMA((2, chips)),
             pltpu.SemaphoreType.DMA((2, 2)),

time: 33.1 us -> 36.1 us (1.091)
  Pallas kernels: 32.2 us -> 35.3 us
    pallas_call x1, Pallas kernels: 32.2 us -> 35.3 us  [fused(): pl.pallas_call(functools.partial(fused_kernel, n_dev), out_shape=pltpu.VM...]
where the time goes in v7:
time: 36.1 us; the launch traced here: 35.9 us
  Pallas kernels  35.3 us (98%)
  local copies, waits for them, and re-layouts  0.61 us (2%)
    pallas_call x1, Pallas kernels, fused(): pl.pallas_call(functools.partial(fused_kernel, n_dev), out_shape=pltpu.VM...  35.3 us

profile of v7, /device:TPU:0, one launch (start us, length us, event | category | flops | bytes accessed | tf_op | source)
XLA Modules:
  0.0 35.9 jit_solution(8576379303942113543)
XLA Ops:
  0.0 35.3 %shard_map.127 = bf16[32,256]{1,0:T(8,128)(2,1)S(1)} custom-call(bf16[2,4096]{1,0:T(2,128)(2,1)} %queries_hbm.1, s32[2]{0:T(128)} %lengths_hbm.1, bf16[32,256]{1,0:T(8,128)(2,1)} %residual_hbm.1, bf16[4096]{0:T(1024)(128)(2,1)} %gain_hbm.1, s32[8,32]{1,0:T(8,128)} %bitcast.2, f32[8,32]{1,0:T(8,128)} %bitcast.3, s32[16]{0:T(128)} %owners_hbm.1, ...), custom_call_target="tpu_custom_call" | custom-call | flops 1375731712 | bytes 42991616 | tf_op jit(solution)/shard_map/pallas_call | solution.py:505
  35.3 0.6 %copy.15 = bf16[32,256]{1,0:T(8,128)(2,1)} copy(bf16[32,256]{1,0:T(8,128)(2,1)S(1)} %shard_map.127) | data formatting | bytes 32768

commit v8 on v5

--- a/solution.py
+++ b/solution.py
@@ -418,7 +418,7 @@
         return made * weight
 
     loads[12].wait()
-    batch = chips // 2
+    batch = chips // 4
 
     def crossing(h):
         part = pl.ds(h * batch, batch)
@@ -433,24 +433,24 @@
             {"dev": 2 * chip_of(k) + core},
         )
 
-    @pl.loop(0, 2)
+    @pl.loop(0, 4)
     def _(step):
-        h = 1 - step
+        h = 3 - step
         for i in range(batch):
             k = h * batch + i
             cross_out[k] = lowered(1 - core, k).astype(jnp.bfloat16)
         crossing(h).start()
 
-    @pl.loop(0, 2)
+    @pl.loop(0, 4)
     def _(step):
-        h = 1 - step
+        h = 3 - step
         made = [lowered(core, h * batch + i) for i in range(batch)]
         crossing(h).wait_recv()
         for i in range(batch):
             k = h * batch + i
             back_out[k] = (made[i] + cross_in[k].astype(jnp.float32)).astype(jnp.bfloat16)
 
-        @pl.loop(h * batch + step, (h + 1) * batch)
+        @pl.loop(h * batch + lax.div(step, 3), (h + 1) * batch)
         def _(k):
             backing(k).start()
 
@@ -461,7 +461,7 @@
     gather_sent(kv_heads, hidden_in)
     swap.wait_send()
 
-    @pl.loop(0, 2)
+    @pl.loop(0, 4)
     def _(h):
         crossing(h).wait_send()
 
@@ -583,7 +583,7 @@
     group = queries.shape[1] // (cache_keys.shape[1] * cache_keys.shape[3])
     return (
         mesh.shape["sec"] == 2
-        and mesh.shape["dev"] in (4, 8, 16)
+        and mesh.shape["dev"] in (8, 16)
         and owners.shape[0] == mesh.shape["dev"]
         and gate_proj.shape[0] == 1
         and group % 16 == 0

time: 33.1 us -> 33.7 us (1.018)
  Pallas kernels: 32.2 us -> 32.8 us
    pallas_call x1, Pallas kernels: 32.2 us -> 32.8 us  [fused(): pl.pallas_call(functools.partial(fused_kernel, n_dev), out_shape=pltpu.VM...]
where the time goes in v8:
time: 33.7 us; the launch traced here: 33.4 us
  Pallas kernels  32.8 us (97%)
  local copies, waits for them, and re-layouts  0.61 us (2%)
    pallas_call x1, Pallas kernels, fused(): pl.pallas_call(functools.partial(fused_kernel, n_dev), out_shape=pltpu.VM...  32.8 us

profile of v8, /device:TPU:0, one launch (start us, length us, event | category | flops | bytes accessed | tf_op | source)
XLA Modules:
  0.0 33.4 jit_solution(8663978775113809317)
XLA Ops:
  0.0 32.8 %shard_map.127 = bf16[32,256]{1,0:T(8,128)(2,1)S(1)} custom-call(bf16[2,4096]{1,0:T(2,128)(2,1)} %queries_hbm.1, s32[2]{0:T(128)} %lengths_hbm.1, bf16[32,256]{1,0:T(8,128)(2,1)} %residual_hbm.1, bf16[4096]{0:T(1024)(128)(2,1)} %gain_hbm.1, s32[8,32]{1,0:T(8,128)} %bitcast.2, f32[8,32]{1,0:T(8,128)} %bitcast.3, s32[16]{0:T(128)} %owners_hbm.1, ...), custom_call_target="tpu_custom_call" | custom-call | flops 1375731712 | bytes 42991616 | tf_op jit(solution)/shard_map/pallas_call | solution.py:529
  32.8 0.6 %copy.15 = bf16[32,256]{1,0:T(8,128)(2,1)} copy(bf16[32,256]{1,0:T(8,128)(2,1)S(1)} %shard_map.127) | data formatting | bytes 32768
